TPU v7x, 32 devices: a whole 2x2x4 slice. The times are simulated.
32 devices in a mesh: px: 4 (over z), py: 4 (over y, core), lev: 2 (over x).
Axes of the slice: x: 2, y: 2, z: 4, core: 2. Of those that a mesh axis runs over, the one named last changes fastest.
Arguments:
- pressure: float32 [8, 512, 512], P('lev', 'px', 'py'), may hold values from -6 to 6
- wind_east: float32 [8, 512, 512], P('lev', 'px', 'py'), may hold values from -6 to 6
- wind_north: float32 [8, 512, 512], P('lev', 'px', 'py'), may hold values from -6 to 6
- wind_up: float32 [8, 512, 512], P('lev', 'px', 'py'), may hold values from -6 to 6
- stiffness: float32 [8, 512, 512], P('lev', 'px', 'py'), may hold values from 0.3 to 1
- edge_table: int32 [4, 4, 4], replicated, may hold values from 0 to 7
- remap_source: int32 [65536], P(('px', 'py')), may hold values from 0 to 16383
- remap_weight: float32 [65536], P(('px', 'py')), may hold values from 0.25 to 1
- remap_owner: int32 [65536, 1], P(('px', 'py')), may hold values from 0 to 3; in each aligned block of 4096 rows (0 to 4095, 4096 to 8191, ...) at most 2048 rows name the same one
- latlon_cell: int32 [131072], P(('px', 'py')), may hold values from 0 to 2047
Outputs:
- final_pressure: float32 [8, 512, 512], P('lev', 'px', 'py')
- latlon_fields: float32 [4, 8, 32768], P(None, 'lev', ('px', 'py'))
Inputs may be any that keep to these rules, and one draw needn't show every extreme that they name: `remap_owner`: among the 4096 entries of one tile no owner is named more than 2048 times, and in every draw some tile names some owner exactly 2048 times.
All inputs are finite; a program needn't handle non-finite values.
Results may differ from a plain program's by a relative error of at most 0.0003.
Values sent between devices are 32-bit elements; how exact they have to be, the bound alone decides.
A program may use at most 64 MiB of HBM per device.

v0:
```python
import jax
import jax.numpy as jnp
from jax import lax
from jax.sharding import PartitionSpec as P

SUBSTEPS = 4


horiz_coef = 0.45
vert_coef = 0.3


def extended_2(cells, sides, width):
    for axis, dim in sides:
        count = lax.axis_size(axis)
        head = lax.slice_in_dim(cells, 0, width, axis=dim)
        tail = lax.slice_in_dim(cells, cells.shape[dim] - width, cells.shape[dim], axis=dim)
        cells = jnp.concatenate(
            [
                lax.ppermute(tail, axis, [(i, (i + 1) % count) for i in range(count)]),
                cells,
                lax.ppermute(head, axis, [((i + 1) % count, i) for i in range(count)]),
            ],
            axis=dim,
        )
    return cells


def shifted(shard, axis, by):
    count = lax.axis_size(axis)
    pairs = [(i, i + by) for i in range(count) if 0 <= i + by < count]
    return lax.ppermute(shard, axis, pairs)


def rim_stack(fields):
    west_rim = fields[:, :, 0, :]
    south_rim = fields[:, :, :, 0]
    east_rim = fields[:, :, -1, :]
    north_rim = fields[:, :, :, -1]
    return jnp.stack([west_rim, south_rim, east_rim, north_rim])


def turn_pair(first, second, quarter_turns):
    new_first = jnp.where(
        quarter_turns == 0,
        first,
        jnp.where(quarter_turns == 1, -second, jnp.where(quarter_turns == 2, -first, second)),
    )
    new_second = jnp.where(
        quarter_turns == 0,
        second,
        jnp.where(quarter_turns == 1, first, jnp.where(quarter_turns == 2, -second, -first)),
    )
    return (new_first, new_second)


def ghost_rims(fields, edge_table, vector):
    index_first = lax.axis_index("px")
    index_second = lax.axis_index("py")
    own_codes = edge_table[index_first, index_second]
    borders = rim_stack(fields)
    nfield = fields.shape[0]
    levels = fields.shape[1]
    tile_cells = fields.shape[2]
    flat_size = nfield * levels * tile_cells
    packet = borders.reshape(1, 1, 4, flat_size)
    extended = extended_2(packet, (("px", 0), ("py", 1)), 1)
    arrived = [extended[0, 1], extended[1, 0], extended[2, 1], extended[1, 2]]
    raw_ghosts = []
    for facing in range(4):
        offered = arrived[facing].reshape(4, nfield, levels, tile_cells)
        wanted = (facing + 2 + own_codes[facing] % 4) % 4
        raw_ghosts.append(offered[wanted])
    result = []
    for facing in range(4):
        quarter_turns = own_codes[facing] % 4
        flipped = own_codes[facing] // 4
        ghost = jnp.where(flipped == 1, raw_ghosts[facing][..., ::-1], raw_ghosts[facing])
        if vector:
            turned_first, turned_second = turn_pair(ghost[0], ghost[1], quarter_turns)
            ghost = jnp.stack([turned_first, turned_second])
        result.append(ghost)
    return result


def spreads(field, ghosts):
    west_ghost, south_ghost, east_ghost, north_ghost = ghosts
    east_val = jnp.concatenate([field[:, 1:, :], east_ghost[:, None, :]], axis=1)
    west_val = jnp.concatenate([west_ghost[:, None, :], field[:, :-1, :]], axis=1)
    north_val = jnp.concatenate([field[:, :, 1:], north_ghost[:, :, None]], axis=2)
    south_val = jnp.concatenate([south_ghost[:, :, None], field[:, :, :-1]], axis=2)
    return (east_val - west_val, north_val - south_val)


def ranking(owner_row, owner_count):
    onehot = (owner_row[:, None] == jnp.arange(owner_count, dtype=jnp.int32)[None, :]).astype(
        jnp.int32
    )
    counts = jnp.cumsum(onehot, axis=0)
    return jnp.sum(counts * onehot, axis=1) - 1


def per_device(
    pressure,
    wind_east,
    wind_north,
    wind_up,
    stiffness,
    edge_table,
    remap_source,
    remap_weight,
    remap_owner,
    latlon_cell,
):
    levels = pressure.shape[0]
    tile_cells = pressure.shape[1]
    level_pos = lax.broadcasted_iota(jnp.int32, pressure.shape, 0)
    summit_mask = (lax.axis_index("lev") == lax.axis_size("lev") - 1) & (level_pos == levels - 1)
    for substep in range(SUBSTEPS):
        press_ghosts = ghost_rims(pressure[None], edge_table, False)
        east_diff, north_diff = spreads(pressure, [ghost[0] for ghost in press_ghosts])
        wind_east = wind_east - horiz_coef * east_diff
        wind_north = wind_north - horiz_coef * north_diff
        from_above = shifted(pressure[:1], "lev", -1)
        press_up = jnp.concatenate([pressure[1:], from_above], axis=0)
        wind_up = jnp.where(summit_mask, 0.0, wind_up - vert_coef * (press_up - pressure))
        from_below = shifted(wind_up[-1:], "lev", 1)
        wind_low = jnp.concatenate([from_below, wind_up[:-1]], axis=0)
        wind_ghosts = ghost_rims(jnp.stack([wind_east, wind_north]), edge_table, True)
        east_flow = spreads(wind_east, [ghost[0] for ghost in wind_ghosts])[0]
        north_flow = spreads(wind_north, [ghost[1] for ghost in wind_ghosts])[1]
        pressure = pressure - stiffness * (
            horiz_coef * (east_flow + north_flow) + vert_coef * (wind_up - wind_low)
        )
    owner_count = lax.axis_size("px")
    slot_count = latlon_cell.shape[0] // owner_count
    cell_count = tile_cells * tile_cells // 8
    fields = jnp.stack([pressure, wind_east, wind_north, wind_up]).reshape(
        4 * levels, tile_cells * tile_cells
    )
    payload = fields[:, remap_source] * remap_weight[None, :]
    owners = remap_owner[:, 0]
    placed_at = owners * slot_count + ranking(owners, owner_count)
    outgoing = (
        jnp.zeros((4 * levels, owner_count * slot_count), jnp.float32).at[:, placed_at].set(payload)
    )
    arrived = lax.all_to_all(outgoing, "px", split_axis=1, concat_axis=1, tiled=True)
    latlon_fields = jnp.zeros((4 * levels, cell_count), jnp.float32).at[:, latlon_cell].add(arrived)
    return (pressure, latlon_fields.reshape(4, levels, cell_count))


def solution(mesh):
    placed = (
        P("lev", "px", "py"),
        P("lev", "px", "py"),
        P("lev", "px", "py"),
        P("lev", "px", "py"),
        P("lev", "px", "py"),
        P(),
        P(("px", "py")),
        P(("px", "py")),
        P(("px", "py"), None),
        P(("px", "py")),
    )
    return jax.shard_map(
        per_device,
        mesh=mesh,
        in_specs=placed,
        out_specs=(P("lev", "px", "py"), P(None, "lev", ("px", "py"))),
        check_vma=False,
    )
```

profile of v0, /device:TPU:0, one launch (start us, length us, event | category | flops | bytes accessed | tf_op | source)
XLA Modules:
  0.0 239.8 jit_solution(91245210602647028)
XLA Ops:
  0.7 1.4 slice_reduce_fusion.7
  2.8 5.1 %collective-permute-start = (f32[1,1,4,512]{3,2,1,0:T(4,128)S(1)}, f32[1,1,4,512]{3,2,1,0:T(4,128)S(1)}, u32[]{:S(2)}, u32[]{:S(2)}) collective-permute-start(f32[1,1,4,512]{3,2,1,0:T(4,128)S(1)} %pad_maximum_fusion.17), channel_id=1, source_target_pairs={{8,0},{16,8},{24,16},{0,24},{9,1},{17,9},{25,17},{1,25},{10,2},{18... | collective-permute-start | bytes 24584 | tf_op jit(solution)/shard_map/ppermute | solution.py:22
  8.8 1.3 collective-permute-start.8
  10.1 1.2 fusion.125
  29.2 1.7 collective-permute-start.2
  33.8 3.9 %collective-permute-start.4 = (f32[1,1,4,1024]{3,2,1,0:T(4,128)S(1)}, f32[1,1,4,1024]{3,2,1,0:T(4,128)S(1)}, u32[]{:S(2)}, u32[]{:S(2)}) collective-permute-start(f32[1,1,4,1024]{3,2,1,0:T(4,128)S(1)} %pad_maximum_fusion.13), channel_id=1, source_target_pairs={{8,0},{16,8},{24,16},{0,24},{9,1},{17,9},{25,17},{1,25},{10,2},{18... | collective-permute-start | bytes 49160 | tf_op jit(solution)/shard_map/ppermute | solution.py:22
  37.8 1.3 collective-permute-done.4
  39.1 4.2 %collective-permute-done.5 = f32[1,1,4,1024]{3,2,1,0:T(4,128)S(1)} collective-permute-done((f32[1,1,4,1024]{3,2,1,0:T(4,128)S(1)}, f32[1,1,4,1024]{3,2,1,0:T(4,128)S(1)}, u32[]{:S(2)}, u32[]{:S(2)}) %collective-permute-start.5) | collective-permute-done | bytes 16416 | tf_op jit(solution)/shard_map/ppermute | solution.py:20
  43.5 1.6 collective-permute-start.6
  45.6 4.5 %collective-permute-start.9 = (f32[1,128,128]{2,1,0:T(8,128)S(1)}, f32[1,128,128]{2,1,0:T(8,128)S(1)}, u32[]{:S(2)}, u32[]{:S(2)}) collective-permute-start(f32[1,128,128]{2,1,0:T(8,128)S(1)} %slice.642), channel_id=1, source_target_pairs={{0,1},{2,3},{4,5},{6,7},{8,9},{10,11},{12,13},{14,15},{16,17},{18,... | collective-permute-start | bytes 196616 | tf_op jit(solution)/shard_map/ppermute | solution.py:32
  50.8 1.2 collective-permute-done.9
  52.7 2.0 collective-permute-start.11
  55.0 1.3 collective-permute-start.18
  56.4 1.9 collective-permute-done.11
  58.3 1.7 collective-permute-start.12
  63.0 2.0 collective-permute-start.15
  65.1 1.6 collective-permute-done.14
  66.7 1.9 collective-permute-done.15
  68.8 1.6 collective-permute-start.16
  70.9 4.5 %collective-permute-start.19 = (f32[1,128,128]{2,1,0:T(8,128)S(1)}, f32[1,128,128]{2,1,0:T(8,128)S(1)}, u32[]{:S(2)}, u32[]{:S(2)}) collective-permute-start(f32[1,128,128]{2,1,0:T(8,128)S(1)} %slice.674), channel_id=1, source_target_pairs={{0,1},{2,3},{4,5},{6,7},{8,9},{10,11},{12,13},{14,15},{16,17},{18,... | collective-permute-start | bytes 196616 | tf_op jit(solution)/shard_map/ppermute | solution.py:32
  76.0 1.2 collective-permute-done.19
  77.9 2.0 collective-permute-start.21
  80.1 1.3 collective-permute-start.28
  81.5 1.9 collective-permute-done.21
  83.5 1.7 collective-permute-start.22
  88.2 2.0 collective-permute-start.25
  90.3 1.6 collective-permute-done.24
  91.9 1.9 collective-permute-done.25
  93.9 1.6 collective-permute-start.26
  96.0 4.5 %collective-permute-start.29 = (f32[1,128,128]{2,1,0:T(8,128)S(1)}, f32[1,128,128]{2,1,0:T(8,128)S(1)}, u32[]{:S(2)}, u32[]{:S(2)}) collective-permute-start(f32[1,128,128]{2,1,0:T(8,128)S(1)} %slice.706), channel_id=1, source_target_pairs={{0,1},{2,3},{4,5},{6,7},{8,9},{10,11},{12,13},{14,15},{16,17},{18,... | collective-permute-start | bytes 196616 | tf_op jit(solution)/shard_map/ppermute | solution.py:32
  101.2 1.2 collective-permute-done.29
  103.1 2.0 collective-permute-start.31
  105.4 1.3 collective-permute-start.38
  106.8 1.9 collective-permute-done.31
  108.7 1.7 collective-permute-start.32
  113.4 2.0 collective-permute-start.35
  115.5 1.7 collective-permute-done.34
  117.2 1.9 collective-permute-done.35
  119.3 1.6 collective-permute-start.36
  121.4 4.5 %collective-permute-start.39 = (f32[1,128,128]{2,1,0:T(8,128)S(1)}, f32[1,128,128]{2,1,0:T(8,128)S(1)}, u32[]{:S(2)}, u32[]{:S(2)}) collective-permute-start(f32[1,128,128]{2,1,0:T(8,128)S(1)} %slice.738), channel_id=1, source_target_pairs={{0,1},{2,3},{4,5},{6,7},{8,9},{10,11},{12,13},{14,15},{16,17},{18,... | collective-permute-start | bytes 196616 | tf_op jit(solution)/shard_map/ppermute | solution.py:32
  126.5 1.2 collective-permute-done.39
  128.7 4.6 %copy.291 = f32[16,16384]{0,1:T(8,128)} copy(f32[16,16384]{1,0:T(8,128)S(1)} %bitcast.408) | data formatting | bytes 2097152 | tf_op jit(solution)/shard_map/reshape | solution.py:138
  133.3 37.8 %scatter_custom_fusion = f32[16,8192]{0,1:T(8,128)} fusion(s32[4096]{0:T(1024)S(1)} %bitcast.465, f32[]{:T(128)} %constant.311.clone.1, f32[4096]{0:T(1024)S(1)} %copy-done.8, f32[16,16384]{0,1:T(8,128)} %copy.291, s32[4096]{0:T(1024)S(1)} %fusion.73), kind=kCustom, calls=%fused_computation.3 | custom fusion | flops 65536 | bytes 1605636 | tf_op jit(solution)/shard_map/scatter | solution.py:145
  171.1 3.5 %copy.292 = f32[16,4,2048]{2,0,1:T(8,128)} copy(f32[16,4,2048]{0,2,1:T(8,128)} %bitcast.389) | data formatting | bytes 1048576 | tf_op jit(solution)/shard_map/all_to_all | solution.py:147
  174.6 3.5 %all-to-all-start = ((f32[16,4,2048]{2,0,1:T(8,128)}), f32[16,4,2048]{2,0,1:T(8,128)S(1)}, u32[]{:S(2)}, u32[]{:S(2)}) async-start(f32[16,4,2048]{2,0,1:T(8,128)} %copy.292), calls=%async_computation | async-start | bytes 1048576 | tf_op jit(solution)/shard_map/all_to_all | solution.py:147
  178.1 13.5 %all-to-all-done = f32[16,4,2048]{2,0,1:T(8,128)S(1)} async-done(((f32[16,4,2048]{2,0,1:T(8,128)}), f32[16,4,2048]{2,0,1:T(8,128)S(1)}, u32[]{:S(2)}, u32[]{:S(2)}) %all-to-all-start) | async-done | bytes 524320 | tf_op jit(solution)/shard_map/all_to_all | solution.py:147
  191.7 2.6 %copy.294 = f32[8192,16]{1,0:T(8,128)} copy(f32[8192,16]{0,1:T(8,128)S(1)} %bitcast.411) | data formatting | bytes 1048576 | tf_op jit(solution)/shard_map/all_to_all | solution.py:147
  194.3 44.6 %scatter_custom_fusion.1 = f32[16,2048]{0,1:T(8,128)S(1)} fusion(s32[8192]{0:T(1024)S(1)} %compare_select_fusion.1, f32[8192,16]{1,0:T(8,128)} %copy.294, f32[]{:T(128)} %constant.311.clone.1), kind=kCustom, calls=%fused_computation.41 | custom fusion | flops 131072 | bytes 131584 | tf_op jit(solution)/shard_map/scatter-add | solution.py:148
  (335 shorter events, 30.7 us)
Async XLA Ops:
  0.6 11.7 %copy-start = (s32[4,4,4]{2,1,0:T(4,128)S(1)}, s32[4,4,4]{2,1,0:T(4,128)}, u32[]{:S(2)}) copy-start(s32[4,4,4]{2,1,0:T(4,128)} %param.15) | copy-start | bytes 772
  0.6 30.5 %copy-start.4 = (f32[4,128,128]{2,1,0:T(8,128)S(1)}, f32[4,128,128]{2,1,0:T(8,128)}, u32[]{:S(2)}) copy-start(f32[4,128,128]{2,1,0:T(8,128)} %param.11) | copy-start | bytes 786436
  0.7 32.4 %copy-start.5 = (f32[4,128,128]{2,1,0:T(8,128)S(1)}, f32[4,128,128]{2,1,0:T(8,128)}, u32[]{:S(2)}) copy-start(f32[4,128,128]{2,1,0:T(8,128)} %param.12) | copy-start | bytes 786436
  2.8 26.3 %collective-permute-start = (f32[1,1,4,512]{3,2,1,0:T(4,128)S(1)}, f32[1,1,4,512]{3,2,1,0:T(4,128)S(1)}, u32[]{:S(2)}, u32[]{:S(2)}) collective-permute-start(f32[1,1,4,512]{3,2,1,0:T(4,128)S(1)} %pad_maximum_fusion.17), channel_id=1, source_target_pairs={{8,0},{16,8},{24,16},{0,24},{9,1},{17,9},{25,17},{1,25},{10,2},{18... | collective-permute-start | bytes 24584 | tf_op jit(solution)/shard_map/ppermute | solution.py:22
  7.9 21.2 %collective-permute-start.1 = (f32[1,1,4,512]{3,2,1,0:T(4,128)S(1)}, f32[1,1,4,512]{3,2,1,0:T(4,128)S(1)}, u32[]{:S(2)}, u32[]{:S(2)}) collective-permute-start(f32[1,1,4,512]{3,2,1,0:T(4,128)S(1)} %pad_maximum_fusion.17), channel_id=1, source_target_pairs={{0,8},{8,16},{16,24},{24,0},{1,9},{9,17},{17,25},{25,1},{2,10},{10... | collective-permute-start | bytes 24584 | tf_op jit(solution)/shard_map/ppermute | solution.py:20
  8.8 36.7 %collective-permute-start.8 = (f32[1,128,128]{2,1,0:T(8,128)S(1)}, f32[1,128,128]{2,1,0:T(8,128)S(1)}, u32[]{:S(2)}, u32[]{:S(2)}) collective-permute-start(f32[1,128,128]{2,1,0:T(8,128)S(1)} %slice.515), channel_id=1, source_target_pairs={{1,0},{3,2},{5,4},{7,6},{9,8},{11,10},{13,12},{15,14},{17,16},{19,... | collective-permute-start | bytes 196616 | tf_op jit(solution)/shard_map/ppermute | solution.py:32
  12.3 33.2 %copy-start.1 = (f32[4,128,128]{2,1,0:T(8,128)S(1)}, f32[4,128,128]{2,1,0:T(8,128)}, u32[]{:S(2)}) copy-start(f32[4,128,128]{2,1,0:T(8,128)} %param.10) | copy-start | bytes 786436
  12.3 33.2 %copy-start.6 = (f32[4,128,128]{2,1,0:T(8,128)S(1)}, f32[4,128,128]{2,1,0:T(8,128)}, u32[]{:S(2)}) copy-start(f32[4,128,128]{2,1,0:T(8,128)} %param.13) | copy-start | bytes 786436
  29.1 3.3 %collective-permute-start.3 = (f32[3,1,4,512]{3,2,1,0:T(4,128)S(1)}, f32[3,1,4,512]{3,2,1,0:T(4,128)S(1)}, u32[]{:S(2)}, u32[]{:S(2)}) collective-permute-start(f32[3,1,4,512]{3,2,1,0:T(4,128)S(1)} %pad_maximum_fusion.9), channel_id=1, source_target_pairs={{0,2},{2,4},{4,6},{6,0},{1,3},{3,5},{5,7},{7,1},{8,10},{10,12},{12... | collective-permute-start | bytes 73736 | tf_op jit(solution)/shard_map/ppermute | solution.py:20
  29.2 3.5 %collective-permute-start.2 = (f32[3,1,4,512]{3,2,1,0:T(4,128)S(1)}, f32[3,1,4,512]{3,2,1,0:T(4,128)S(1)}, u32[]{:S(2)}, u32[]{:S(2)}) collective-permute-start(f32[3,1,4,512]{3,2,1,0:T(4,128)S(1)} %pad_maximum_fusion.9), channel_id=1, source_target_pairs={{2,0},{4,2},{6,4},{0,6},{3,1},{5,3},{7,5},{1,7},{10,8},{12,10},{14... | collective-permute-start | bytes 73736 | tf_op jit(solution)/shard_map/ppermute | solution.py:22
  31.2 20.8 %copy-start.2 = (f32[4,128,128]{2,1,0:T(8,128)S(1)}, f32[4,128,128]{2,1,0:T(8,128)}, u32[]{:S(2)}) copy-start(f32[4,128,128]{2,1,0:T(8,128)} %param.14) | copy-start | bytes 786436
  33.8 5.3 %collective-permute-start.4 = (f32[1,1,4,1024]{3,2,1,0:T(4,128)S(1)}, f32[1,1,4,1024]{3,2,1,0:T(4,128)S(1)}, u32[]{:S(2)}, u32[]{:S(2)}) collective-permute-start(f32[1,1,4,1024]{3,2,1,0:T(4,128)S(1)} %pad_maximum_fusion.13), channel_id=1, source_target_pairs={{8,0},{16,8},{24,16},{0,24},{9,1},{17,9},{25,17},{1,25},{10,2},{18... | collective-permute-start | bytes 49160 | tf_op jit(solution)/shard_map/ppermute | solution.py:22
  37.7 5.6 %collective-permute-start.5 = (f32[1,1,4,1024]{3,2,1,0:T(4,128)S(1)}, f32[1,1,4,1024]{3,2,1,0:T(4,128)S(1)}, u32[]{:S(2)}, u32[]{:S(2)}) collective-permute-start(f32[1,1,4,1024]{3,2,1,0:T(4,128)S(1)} %pad_maximum_fusion.13), channel_id=1, source_target_pairs={{0,8},{8,16},{16,24},{24,0},{1,9},{9,17},{17,25},{25,1},{2,10},{10... | collective-permute-start | bytes 49160 | tf_op jit(solution)/shard_map/ppermute | solution.py:20
  43.3 6.8 %collective-permute-start.7 = (f32[3,1,4,1024]{3,2,1,0:T(4,128)S(1)}, f32[3,1,4,1024]{3,2,1,0:T(4,128)S(1)}, u32[]{:S(2)}, u32[]{:S(2)}) collective-permute-start(f32[3,1,4,1024]{3,2,1,0:T(4,128)S(1)} %pad_maximum_fusion.5), channel_id=1, source_target_pairs={{0,2},{2,4},{4,6},{6,0},{1,3},{3,5},{5,7},{7,1},{8,10},{10,12},{12... | collective-permute-start | bytes 147464 | tf_op jit(solution)/shard_map/ppermute | solution.py:20
  43.5 6.8 %collective-permute-start.6 = (f32[3,1,4,1024]{3,2,1,0:T(4,128)S(1)}, f32[3,1,4,1024]{3,2,1,0:T(4,128)S(1)}, u32[]{:S(2)}, u32[]{:S(2)}) collective-permute-start(f32[3,1,4,1024]{3,2,1,0:T(4,128)S(1)} %pad_maximum_fusion.5), channel_id=1, source_target_pairs={{2,0},{4,2},{6,4},{0,6},{3,1},{5,3},{7,5},{1,7},{10,8},{12,10},{14... | collective-permute-start | bytes 147464 | tf_op jit(solution)/shard_map/ppermute | solution.py:22
  45.6 6.4 %collective-permute-start.9 = (f32[1,128,128]{2,1,0:T(8,128)S(1)}, f32[1,128,128]{2,1,0:T(8,128)S(1)}, u32[]{:S(2)}, u32[]{:S(2)}) collective-permute-start(f32[1,128,128]{2,1,0:T(8,128)S(1)} %slice.642), channel_id=1, source_target_pairs={{0,1},{2,3},{4,5},{6,7},{8,9},{10,11},{12,13},{14,15},{16,17},{18,... | collective-permute-start | bytes 196616 | tf_op jit(solution)/shard_map/ppermute | solution.py:32
  52.7 3.7 %collective-permute-start.10 = (f32[1,1,4,512]{3,2,1,0:T(4,128)S(1)}, f32[1,1,4,512]{3,2,1,0:T(4,128)S(1)}, u32[]{:S(2)}, u32[]{:S(2)}) collective-permute-start(f32[1,1,4,512]{3,2,1,0:T(4,128)S(1)} %pad_maximum_fusion.18), channel_id=1, source_target_pairs={{8,0},{16,8},{24,16},{0,24},{9,1},{17,9},{25,17},{1,25},{10,2},{18... | collective-permute-start | bytes 24584 | tf_op jit(solution)/shard_map/ppermute | solution.py:22
  52.7 5.5 %collective-permute-start.11 = (f32[1,1,4,512]{3,2,1,0:T(4,128)S(1)}, f32[1,1,4,512]{3,2,1,0:T(4,128)S(1)}, u32[]{:S(2)}, u32[]{:S(2)}) collective-permute-start(f32[1,1,4,512]{3,2,1,0:T(4,128)S(1)} %pad_maximum_fusion.18), channel_id=1, source_target_pairs={{0,8},{8,16},{16,24},{24,0},{1,9},{9,17},{17,25},{25,1},{2,10},{10... | collective-permute-start | bytes 24584 | tf_op jit(solution)/shard_map/ppermute | solution.py:20
  55.0 15.8 %collective-permute-start.18 = (f32[1,128,128]{2,1,0:T(8,128)S(1)}, f32[1,128,128]{2,1,0:T(8,128)S(1)}, u32[]{:S(2)}, u32[]{:S(2)}) collective-permute-start(f32[1,128,128]{2,1,0:T(8,128)S(1)} %slice.673), channel_id=1, source_target_pairs={{1,0},{3,2},{5,4},{7,6},{9,8},{11,10},{13,12},{15,14},{17,16},{19,... | collective-permute-start | bytes 196616 | tf_op jit(solution)/shard_map/ppermute | solution.py:32
  58.3 3.3 %collective-permute-start.13 = (f32[3,1,4,512]{3,2,1,0:T(4,128)S(1)}, f32[3,1,4,512]{3,2,1,0:T(4,128)S(1)}, u32[]{:S(2)}, u32[]{:S(2)}) collective-permute-start(f32[3,1,4,512]{3,2,1,0:T(4,128)S(1)} %pad_maximum_fusion.10), channel_id=1, source_target_pairs={{0,2},{2,4},{4,6},{6,0},{1,3},{3,5},{5,7},{7,1},{8,10},{10,12},{12... | collective-permute-start | bytes 73736 | tf_op jit(solution)/shard_map/ppermute | solution.py:20
  58.3 3.5 %collective-permute-start.12 = (f32[3,1,4,512]{3,2,1,0:T(4,128)S(1)}, f32[3,1,4,512]{3,2,1,0:T(4,128)S(1)}, u32[]{:S(2)}, u32[]{:S(2)}) collective-permute-start(f32[3,1,4,512]{3,2,1,0:T(4,128)S(1)} %pad_maximum_fusion.10), channel_id=1, source_target_pairs={{2,0},{4,2},{6,4},{0,6},{3,1},{5,3},{7,5},{1,7},{10,8},{12,10},{14... | collective-permute-start | bytes 73736 | tf_op jit(solution)/shard_map/ppermute | solution.py:22
  62.9 3.8 %collective-permute-start.14 = (f32[1,1,4,1024]{3,2,1,0:T(4,128)S(1)}, f32[1,1,4,1024]{3,2,1,0:T(4,128)S(1)}, u32[]{:S(2)}, u32[]{:S(2)}) collective-permute-start(f32[1,1,4,1024]{3,2,1,0:T(4,128)S(1)} %pad_maximum_fusion.14), channel_id=1, source_target_pairs={{8,0},{16,8},{24,16},{0,24},{9,1},{17,9},{25,17},{1,25},{10,2},{18... | collective-permute-start | bytes 49160 | tf_op jit(solution)/shard_map/ppermute | solution.py:22
  63.0 5.6 %collective-permute-start.15 = (f32[1,1,4,1024]{3,2,1,0:T(4,128)S(1)}, f32[1,1,4,1024]{3,2,1,0:T(4,128)S(1)}, u32[]{:S(2)}, u32[]{:S(2)}) collective-permute-start(f32[1,1,4,1024]{3,2,1,0:T(4,128)S(1)} %pad_maximum_fusion.14), channel_id=1, source_target_pairs={{0,8},{8,16},{16,24},{24,0},{1,9},{9,17},{17,25},{25,1},{2,10},{10... | collective-permute-start | bytes 49160 | tf_op jit(solution)/shard_map/ppermute | solution.py:20
  68.6 6.7 %collective-permute-start.17 = (f32[3,1,4,1024]{3,2,1,0:T(4,128)S(1)}, f32[3,1,4,1024]{3,2,1,0:T(4,128)S(1)}, u32[]{:S(2)}, u32[]{:S(2)}) collective-permute-start(f32[3,1,4,1024]{3,2,1,0:T(4,128)S(1)} %pad_maximum_fusion.6), channel_id=1, source_target_pairs={{0,2},{2,4},{4,6},{6,0},{1,3},{3,5},{5,7},{7,1},{8,10},{10,12},{12... | collective-permute-start | bytes 147464 | tf_op jit(solution)/shard_map/ppermute | solution.py:20
  68.8 6.7 %collective-permute-start.16 = (f32[3,1,4,1024]{3,2,1,0:T(4,128)S(1)}, f32[3,1,4,1024]{3,2,1,0:T(4,128)S(1)}, u32[]{:S(2)}, u32[]{:S(2)}) collective-permute-start(f32[3,1,4,1024]{3,2,1,0:T(4,128)S(1)} %pad_maximum_fusion.6), channel_id=1, source_target_pairs={{2,0},{4,2},{6,4},{0,6},{3,1},{5,3},{7,5},{1,7},{10,8},{12,10},{14... | collective-permute-start | bytes 147464 | tf_op jit(solution)/shard_map/ppermute | solution.py:22
  70.9 6.3 %collective-permute-start.19 = (f32[1,128,128]{2,1,0:T(8,128)S(1)}, f32[1,128,128]{2,1,0:T(8,128)S(1)}, u32[]{:S(2)}, u32[]{:S(2)}) collective-permute-start(f32[1,128,128]{2,1,0:T(8,128)S(1)} %slice.674), channel_id=1, source_target_pairs={{0,1},{2,3},{4,5},{6,7},{8,9},{10,11},{12,13},{14,15},{16,17},{18,... | collective-permute-start | bytes 196616 | tf_op jit(solution)/shard_map/ppermute | solution.py:32
  77.8 3.7 %collective-permute-start.20 = (f32[1,1,4,512]{3,2,1,0:T(4,128)S(1)}, f32[1,1,4,512]{3,2,1,0:T(4,128)S(1)}, u32[]{:S(2)}, u32[]{:S(2)}) collective-permute-start(f32[1,1,4,512]{3,2,1,0:T(4,128)S(1)} %pad_maximum_fusion.19), channel_id=1, source_target_pairs={{8,0},{16,8},{24,16},{0,24},{9,1},{17,9},{25,17},{1,25},{10,2},{18... | collective-permute-start | bytes 24584 | tf_op jit(solution)/shard_map/ppermute | solution.py:22
  77.9 5.5 %collective-permute-start.21 = (f32[1,1,4,512]{3,2,1,0:T(4,128)S(1)}, f32[1,1,4,512]{3,2,1,0:T(4,128)S(1)}, u32[]{:S(2)}, u32[]{:S(2)}) collective-permute-start(f32[1,1,4,512]{3,2,1,0:T(4,128)S(1)} %pad_maximum_fusion.19), channel_id=1, source_target_pairs={{0,8},{8,16},{16,24},{24,0},{1,9},{9,17},{17,25},{25,1},{2,10},{10... | collective-permute-start | bytes 24584 | tf_op jit(solution)/shard_map/ppermute | solution.py:20
  80.1 15.8 %collective-permute-start.28 = (f32[1,128,128]{2,1,0:T(8,128)S(1)}, f32[1,128,128]{2,1,0:T(8,128)S(1)}, u32[]{:S(2)}, u32[]{:S(2)}) collective-permute-start(f32[1,128,128]{2,1,0:T(8,128)S(1)} %slice.705), channel_id=1, source_target_pairs={{1,0},{3,2},{5,4},{7,6},{9,8},{11,10},{13,12},{15,14},{17,16},{19,... | collective-permute-start | bytes 196616 | tf_op jit(solution)/shard_map/ppermute | solution.py:32
  83.4 3.3 %collective-permute-start.23 = (f32[3,1,4,512]{3,2,1,0:T(4,128)S(1)}, f32[3,1,4,512]{3,2,1,0:T(4,128)S(1)}, u32[]{:S(2)}, u32[]{:S(2)}) collective-permute-start(f32[3,1,4,512]{3,2,1,0:T(4,128)S(1)} %pad_maximum_fusion.11), channel_id=1, source_target_pairs={{0,2},{2,4},{4,6},{6,0},{1,3},{3,5},{5,7},{7,1},{8,10},{10,12},{12... | collective-permute-start | bytes 73736 | tf_op jit(solution)/shard_map/ppermute | solution.py:20
  83.5 3.5 %collective-permute-start.22 = (f32[3,1,4,512]{3,2,1,0:T(4,128)S(1)}, f32[3,1,4,512]{3,2,1,0:T(4,128)S(1)}, u32[]{:S(2)}, u32[]{:S(2)}) collective-permute-start(f32[3,1,4,512]{3,2,1,0:T(4,128)S(1)} %pad_maximum_fusion.11), channel_id=1, source_target_pairs={{2,0},{4,2},{6,4},{0,6},{3,1},{5,3},{7,5},{1,7},{10,8},{12,10},{14... | collective-permute-start | bytes 73736 | tf_op jit(solution)/shard_map/ppermute | solution.py:22
  88.1 3.8 %collective-permute-start.24 = (f32[1,1,4,1024]{3,2,1,0:T(4,128)S(1)}, f32[1,1,4,1024]{3,2,1,0:T(4,128)S(1)}, u32[]{:S(2)}, u32[]{:S(2)}) collective-permute-start(f32[1,1,4,1024]{3,2,1,0:T(4,128)S(1)} %pad_maximum_fusion.15), channel_id=1, source_target_pairs={{8,0},{16,8},{24,16},{0,24},{9,1},{17,9},{25,17},{1,25},{10,2},{18... | collective-permute-start | bytes 49160 | tf_op jit(solution)/shard_map/ppermute | solution.py:22
  88.2 5.6 %collective-permute-start.25 = (f32[1,1,4,1024]{3,2,1,0:T(4,128)S(1)}, f32[1,1,4,1024]{3,2,1,0:T(4,128)S(1)}, u32[]{:S(2)}, u32[]{:S(2)}) collective-permute-start(f32[1,1,4,1024]{3,2,1,0:T(4,128)S(1)} %pad_maximum_fusion.15), channel_id=1, source_target_pairs={{0,8},{8,16},{16,24},{24,0},{1,9},{9,17},{17,25},{25,1},{2,10},{10... | collective-permute-start | bytes 49160 | tf_op jit(solution)/shard_map/ppermute | solution.py:20
  93.8 6.8 %collective-permute-start.27 = (f32[3,1,4,1024]{3,2,1,0:T(4,128)S(1)}, f32[3,1,4,1024]{3,2,1,0:T(4,128)S(1)}, u32[]{:S(2)}, u32[]{:S(2)}) collective-permute-start(f32[3,1,4,1024]{3,2,1,0:T(4,128)S(1)} %pad_maximum_fusion.7), channel_id=1, source_target_pairs={{0,2},{2,4},{4,6},{6,0},{1,3},{3,5},{5,7},{7,1},{8,10},{10,12},{12... | collective-permute-start | bytes 147464 | tf_op jit(solution)/shard_map/ppermute | solution.py:20
  93.9 6.8 %collective-permute-start.26 = (f32[3,1,4,1024]{3,2,1,0:T(4,128)S(1)}, f32[3,1,4,1024]{3,2,1,0:T(4,128)S(1)}, u32[]{:S(2)}, u32[]{:S(2)}) collective-permute-start(f32[3,1,4,1024]{3,2,1,0:T(4,128)S(1)} %pad_maximum_fusion.7), channel_id=1, source_target_pairs={{2,0},{4,2},{6,4},{0,6},{3,1},{5,3},{7,5},{1,7},{10,8},{12,10},{14... | collective-permute-start | bytes 147464 | tf_op jit(solution)/shard_map/ppermute | solution.py:22
  96.0 6.4 %collective-permute-start.29 = (f32[1,128,128]{2,1,0:T(8,128)S(1)}, f32[1,128,128]{2,1,0:T(8,128)S(1)}, u32[]{:S(2)}, u32[]{:S(2)}) collective-permute-start(f32[1,128,128]{2,1,0:T(8,128)S(1)} %slice.706), channel_id=1, source_target_pairs={{0,1},{2,3},{4,5},{6,7},{8,9},{10,11},{12,13},{14,15},{16,17},{18,... | collective-permute-start | bytes 196616 | tf_op jit(solution)/shard_map/ppermute | solution.py:32
  103.1 3.7 %collective-permute-start.30 = (f32[1,1,4,512]{3,2,1,0:T(4,128)S(1)}, f32[1,1,4,512]{3,2,1,0:T(4,128)S(1)}, u32[]{:S(2)}, u32[]{:S(2)}) collective-permute-start(f32[1,1,4,512]{3,2,1,0:T(4,128)S(1)} %pad_maximum_fusion.20), channel_id=1, source_target_pairs={{8,0},{16,8},{24,16},{0,24},{9,1},{17,9},{25,17},{1,25},{10,2},{18... | collective-permute-start | bytes 24584 | tf_op jit(solution)/shard_map/ppermute | solution.py:22
  103.1 5.5 %collective-permute-start.31 = (f32[1,1,4,512]{3,2,1,0:T(4,128)S(1)}, f32[1,1,4,512]{3,2,1,0:T(4,128)S(1)}, u32[]{:S(2)}, u32[]{:S(2)}) collective-permute-start(f32[1,1,4,512]{3,2,1,0:T(4,128)S(1)} %pad_maximum_fusion.20), channel_id=1, source_target_pairs={{0,8},{8,16},{16,24},{24,0},{1,9},{9,17},{17,25},{25,1},{2,10},{10... | collective-permute-start | bytes 24584 | tf_op jit(solution)/shard_map/ppermute | solution.py:20
  105.4 15.9 %collective-permute-start.38 = (f32[1,128,128]{2,1,0:T(8,128)S(1)}, f32[1,128,128]{2,1,0:T(8,128)S(1)}, u32[]{:S(2)}, u32[]{:S(2)}) collective-permute-start(f32[1,128,128]{2,1,0:T(8,128)S(1)} %slice.737), channel_id=1, source_target_pairs={{1,0},{3,2},{5,4},{7,6},{9,8},{11,10},{13,12},{15,14},{17,16},{19,... | collective-permute-start | bytes 196616 | tf_op jit(solution)/shard_map/ppermute | solution.py:32
  108.7 3.3 %collective-permute-start.33 = (f32[3,1,4,512]{3,2,1,0:T(4,128)S(1)}, f32[3,1,4,512]{3,2,1,0:T(4,128)S(1)}, u32[]{:S(2)}, u32[]{:S(2)}) collective-permute-start(f32[3,1,4,512]{3,2,1,0:T(4,128)S(1)} %pad_maximum_fusion.12), channel_id=1, source_target_pairs={{0,2},{2,4},{4,6},{6,0},{1,3},{3,5},{5,7},{7,1},{8,10},{10,12},{12... | collective-permute-start | bytes 73736 | tf_op jit(solution)/shard_map/ppermute | solution.py:20
  108.7 3.5 %collective-permute-start.32 = (f32[3,1,4,512]{3,2,1,0:T(4,128)S(1)}, f32[3,1,4,512]{3,2,1,0:T(4,128)S(1)}, u32[]{:S(2)}, u32[]{:S(2)}) collective-permute-start(f32[3,1,4,512]{3,2,1,0:T(4,128)S(1)} %pad_maximum_fusion.12), channel_id=1, source_target_pairs={{2,0},{4,2},{6,4},{0,6},{3,1},{5,3},{7,5},{1,7},{10,8},{12,10},{14... | collective-permute-start | bytes 73736 | tf_op jit(solution)/shard_map/ppermute | solution.py:22
  113.3 3.9 %collective-permute-start.34 = (f32[1,1,4,1024]{3,2,1,0:T(4,128)S(1)}, f32[1,1,4,1024]{3,2,1,0:T(4,128)S(1)}, u32[]{:S(2)}, u32[]{:S(2)}) collective-permute-start(f32[1,1,4,1024]{3,2,1,0:T(4,128)S(1)} %pad_maximum_fusion.16), channel_id=1, source_target_pairs={{8,0},{16,8},{24,16},{0,24},{9,1},{17,9},{25,17},{1,25},{10,2},{18... | collective-permute-start | bytes 49160 | tf_op jit(solution)/shard_map/ppermute | solution.py:22
  113.4 5.7 %collective-permute-start.35 = (f32[1,1,4,1024]{3,2,1,0:T(4,128)S(1)}, f32[1,1,4,1024]{3,2,1,0:T(4,128)S(1)}, u32[]{:S(2)}, u32[]{:S(2)}) collective-permute-start(f32[1,1,4,1024]{3,2,1,0:T(4,128)S(1)} %pad_maximum_fusion.16), channel_id=1, source_target_pairs={{0,8},{8,16},{16,24},{24,0},{1,9},{9,17},{17,25},{25,1},{2,10},{10... | collective-permute-start | bytes 49160 | tf_op jit(solution)/shard_map/ppermute | solution.py:20
  119.1 6.7 %collective-permute-start.37 = (f32[3,1,4,1024]{3,2,1,0:T(4,128)S(1)}, f32[3,1,4,1024]{3,2,1,0:T(4,128)S(1)}, u32[]{:S(2)}, u32[]{:S(2)}) collective-permute-start(f32[3,1,4,1024]{3,2,1,0:T(4,128)S(1)} %pad_maximum_fusion.8), channel_id=1, source_target_pairs={{0,2},{2,4},{4,6},{6,0},{1,3},{3,5},{5,7},{7,1},{8,10},{10,12},{12... | collective-permute-start | bytes 147464 | tf_op jit(solution)/shard_map/ppermute | solution.py:20
  119.3 6.7 %collective-permute-start.36 = (f32[3,1,4,1024]{3,2,1,0:T(4,128)S(1)}, f32[3,1,4,1024]{3,2,1,0:T(4,128)S(1)}, u32[]{:S(2)}, u32[]{:S(2)}) collective-permute-start(f32[3,1,4,1024]{3,2,1,0:T(4,128)S(1)} %pad_maximum_fusion.8), channel_id=1, source_target_pairs={{2,0},{4,2},{6,4},{0,6},{3,1},{5,3},{7,5},{1,7},{10,8},{12,10},{14... | collective-permute-start | bytes 147464 | tf_op jit(solution)/shard_map/ppermute | solution.py:22
  121.4 6.3 %collective-permute-start.39 = (f32[1,128,128]{2,1,0:T(8,128)S(1)}, f32[1,128,128]{2,1,0:T(8,128)S(1)}, u32[]{:S(2)}, u32[]{:S(2)}) collective-permute-start(f32[1,128,128]{2,1,0:T(8,128)S(1)} %slice.738), channel_id=1, source_target_pairs={{0,1},{2,3},{4,5},{6,7},{8,9},{10,11},{12,13},{14,15},{16,17},{18,... | collective-permute-start | bytes 196616 | tf_op jit(solution)/shard_map/ppermute | solution.py:32
  171.1 7.0 %copy-start.7 = (s32[8192]{0:T(1024)S(1)}, s32[8192]{0:T(1024)}, u32[]{:S(2)}) copy-start(s32[8192]{0:T(1024)} %param.19) | copy-start | bytes 98308
  174.6 17.0 %all-to-all-start = ((f32[16,4,2048]{2,0,1:T(8,128)}), f32[16,4,2048]{2,0,1:T(8,128)S(1)}, u32[]{:S(2)}, u32[]{:S(2)}) async-start(f32[16,4,2048]{2,0,1:T(8,128)} %copy.292), calls=%async_computation | async-start | bytes 1048576 | tf_op jit(solution)/shard_map/all_to_all | solution.py:147
  (2 other events, 10.0 us)
where the time goes:
time: 241 us; the launch traced here: 240 us
  other arithmetic  92.2 us (38%)
  starting transfers between devices  62.4 us (26%)
  waiting for transfers between devices  44.8 us (19%)
  local copies, waits for them, and re-layouts  28 us (12%)
  between operations  12.5 us (5%)
    scatter-add x1, other arithmetic, per_device(): jnp.zeros((4 * levels, cell_count), jnp.float32).at[:, latlon_cell]  44.6 us
    scatter x1, other arithmetic, per_device(): jnp.zeros((4 * levels, owner_count * slot_count), jnp.float32)  37.8 us
    ppermute x8, starting transfers between devices, shifted(): return lax.ppermute(shard, axis, pairs)  23.1 us
    ppermute x16, starting transfers between devices, extended_2(): lax.ppermute(head, axis, [((i + 1) % count, i) for i in range(count)])  22.8 us
    ppermute x16, waiting for transfers between devices, extended_2(): lax.ppermute(tail, axis, [(i, (i + 1) % count) for i in range(count)])  20 us
    all_to_all x1, waiting for transfers between devices, per_device(): lax.all_to_all(outgoing, 'px', split_axis=1, concat_axis=1, tiled=True)  13.5 us
    ppermute x16, starting transfers between devices, extended_2(): lax.ppermute(tail, axis, [(i, (i + 1) % count) for i in range(count)])  13 us
    ppermute x16, waiting for transfers between devices, extended_2(): lax.ppermute(head, axis, [((i + 1) % count, i) for i in range(count)])  6.46 us
  transfers between devices with their start and end apart: 41, of which 23 were waited for; matrix products, arithmetic and copies ran while one was open for 9% of the time, Pallas kernels for 0%

commit v1 on v0

v1 whole, which is shorter than its diff:
```python
import functools

import jax
import jax.numpy as jnp
from jax import lax
from jax.experimental import pallas as pl
from jax.experimental.pallas import tpu as pltpu
from jax.sharding import PartitionSpec as P

SUBSTEPS = 4
A = 0.45
B = 0.3
LANES = 128
BLOCK = 256
MESH = pl.DeviceIdType.MESH


def iota(shape, dim):
    return lax.broadcasted_iota(jnp.int32, shape, dim)


def parts2(x):
    high = x.astype(jnp.bfloat16)
    return high, (x - high.astype(jnp.float32)).astype(jnp.bfloat16)


def dot_nt(a, b):
    return lax.dot_general(a, b, (((1,), (1,)), ((), ())), preferred_element_type=jnp.float32)


def substeps_kernel(
    sizes,
    edges,
    p_in,
    we_in,
    wn_in,
    wu_in,
    st,
    p,
    we,
    wn,
    wu,
    psend,
    precv,
    wsend,
    wrecv,
    above,
    below,
    wu_below,
    flipped_cols,
    ghost_rows,
    pre,
    st_rims,
    psend_sem,
    precv_sem,
    wsend_sem,
    wrecv_sem,
    up_sems,
    down_sems,
    wub_sems,
):
    n_px, n_py, n_lev = sizes
    levels, tile, _ = p_in.shape
    last = tile - 1
    ix, iy, iz = lax.axis_index("px"), lax.axis_index("py"), lax.axis_index("lev")
    targets = (
        {"px": lax.rem(ix + 1, n_px)},
        {"py": lax.rem(iy + 1, n_py)},
        {"px": lax.rem(ix + n_px - 1, n_px)},
        {"py": lax.rem(iy + n_py - 1, n_py)},
    )
    has_above, has_below = iz < n_lev - 1, iz > 0

    barrier = pltpu.get_barrier_semaphore()
    for target in targets:
        pl.semaphore_signal(barrier, inc=1, device_id=target, device_id_type=MESH)

    @pl.when(has_above)
    def _():
        pl.semaphore_signal(barrier, inc=1, device_id={"lev": iz + 1}, device_id_type=MESH)

    @pl.when(has_below)
    def _():
        pl.semaphore_signal(barrier, inc=1, device_id={"lev": iz - 1}, device_id_type=MESH)

    def rim_copy(send, recv, send_sem, recv_sem, t, s):
        return pltpu.make_async_remote_copy(
            src_ref=send.at[t],
            dst_ref=recv.at[t, s],
            send_sem=send_sem.at[t, s],
            recv_sem=recv_sem.at[t, s],
            device_id=targets[s],
            device_id_type=MESH,
        )

    p_copy = functools.partial(rim_copy, psend, precv, psend_sem, precv_sem)
    w_copy = functools.partial(rim_copy, wsend, wrecv, wsend_sem, wrecv_sem)

    def up_copy(t):
        return pltpu.make_async_remote_copy(
            src_ref=p.at[levels - 1],
            dst_ref=below.at[t],
            send_sem=up_sems.at[0, t],
            recv_sem=up_sems.at[1, t],
            device_id={"lev": iz + 1},
            device_id_type=MESH,
        )

    def down_copy(t):
        return pltpu.make_async_remote_copy(
            src_ref=p.at[0],
            dst_ref=above.at[t],
            send_sem=down_sems.at[0, t],
            recv_sem=down_sems.at[1, t],
            device_id={"lev": iz - 1},
            device_id_type=MESH,
        )

    def wub_copy():
        return pltpu.make_async_remote_copy(
            src_ref=wu_in.at[levels - 1],
            dst_ref=wu_below,
            send_sem=wub_sems.at[0],
            recv_sem=wub_sems.at[1],
            device_id={"lev": iz + 1},
            device_id_type=MESH,
        )

    row, lane = iota((tile, tile), 0), iota((tile, tile), 1)
    edge_lanes = (lane == 0) | (lane == last)
    rim_lane = iota((levels, tile), 1)
    first_lane, last_lane = rim_lane == 0, rim_lane == last

    def d_rows(f):
        return jnp.where(row == last, 0.0, pltpu.roll(f, last, 0)) - jnp.where(
            row == 0, 0.0, pltpu.roll(f, 1, 0)
        )

    def d_lanes(f):
        return jnp.where(lane == last, 0.0, pltpu.roll(f, last, 1)) - jnp.where(
            lane == 0, 0.0, pltpu.roll(f, 1, 1)
        )

    def columns(fields):
        packed = jnp.zeros((tile, tile), jnp.float32)
        for j, f in enumerate(fields):
            packed = jnp.where((lane >> 1) == j, pltpu.roll(f, 2 * j + 1, 1), packed)
        flipped_cols[...] = packed.T
        count = len(fields)
        return (
            flipped_cols[pl.ds(1, count, stride=2), :],
            flipped_cols[pl.ds(0, count, stride=2), :],
        )

    def lane_terms(south, north):
        ghost_rows[pl.ds(0, levels, stride=2), :] = north
        ghost_rows[pl.ds(1, levels, stride=2), :] = south
        turned = ghost_rows[...].T
        return [
            jnp.where(edge_lanes, pltpu.roll(turned, (tile - 2 * j - 1) % tile, 1), 0.0)
            for j in range(levels)
        ]

    codes = [edges[ix, iy, s] for s in range(4)]
    turns = [c & 3 for c in codes]
    wanted = [(s + 2 + turns[s]) & 3 for s in range(4)]
    place = iota((2 * levels, tile), 1)
    order = [jnp.where((codes[s] >> 2) == 1, last - place, place) for s in range(4)]
    low = iota((2 * levels, tile), 0) < levels

    def picked_rim(recv, t, s):
        rim = recv[t, s, 0]
        for k in range(1, 4):
            rim = jnp.where(wanted[s] == k, recv[t, s, k], rim)
        return rim

    def pressure_ghosts(t):
        ghosts = []
        for s in (0, 2):
            for k in (s, s + 1):
                p_copy(t, k).wait_recv()
            both = jnp.concatenate([picked_rim(precv, t, s), picked_rim(precv, t, s + 1)], axis=0)
            both = jnp.take_along_axis(both, jnp.where(low, order[s], order[s + 1]), axis=1)
            ghosts += [both[:levels], both[levels:]]
        return ghosts

    def wind_ghosts(t):
        ghosts = []
        for s in range(4):
            w_copy(t, s).wait_recv()
            both = jnp.take_along_axis(picked_rim(wrecv, t, s), order[s], axis=1)
            a, b = both[:levels], both[levels:]
            r = turns[s]
            if s % 2 == 0:
                ghost = jnp.where(r == 0, a, jnp.where(r == 1, -b, jnp.where(r == 2, -a, b)))
            else:
                ghost = jnp.where(r == 0, b, jnp.where(r == 1, a, jnp.where(r == 2, -b, -a)))
            ghosts.append(ghost)
        return ghosts

    def corner(first, second, end):
        if end == 0:
            return jnp.where(first_lane, first, 0.0) - jnp.where(last_lane, pltpu.roll(second, last, 1), 0.0)
        return jnp.where(first_lane, pltpu.roll(first, 1, 1), 0.0) - jnp.where(last_lane, second, 0.0)

    p[...] = p_in[...]
    south, north = columns([p_in[j] for j in range(levels)])
    psend[0, 0] = p_in[:, 0, :]
    psend[0, 1] = south
    psend[0, 2] = p_in[:, last, :]
    psend[0, 3] = north

    pl.semaphore_wait(barrier, 4 + has_above.astype(jnp.int32) + has_below.astype(jnp.int32))
    for s in range(4):
        p_copy(0, s).start()

    @pl.when(has_above)
    def _():
        wub_copy().start()

    @pl.when(jnp.logical_not(has_below))
    def _():
        wu_below[...] = jnp.zeros((tile, tile), jnp.float32)

    ghost_rows[...] = jnp.zeros((tile, tile), jnp.float32)
    south, north = columns([st[j] for j in range(levels)])
    st_rims[0] = st[:, 0, :] * A
    st_rims[1] = south * A
    st_rims[2] = st[:, last, :] * A
    st_rims[3] = north * A
    we[...] = we_in[...]
    wn[...] = wn_in[...]
    wu[...] = wu_in[...]

    def substep(t, carry):
        @pl.when(has_above)
        def _():
            up_copy(t).start()

        @pl.when(has_below)
        def _():
            down_copy(t).start()

        for j in range(levels):
            we[j] = we[j] - A * d_rows(p[j])
            wn[j] = wn[j] - A * d_lanes(p[j])
        south, north = columns([we[j] for j in range(levels)] + [wn[j] for j in range(levels)])
        pre[0, :levels] = we[:, 0, :]
        pre[0, levels:] = wn[:, 0, :]
        pre[1] = south
        pre[2, :levels] = we[:, last, :]
        pre[2, levels:] = wn[:, last, :]
        pre[3] = north
        for j in range(levels - 1):
            wu[j] = wu[j] - B * (p[j + 1] - p[j])

        gw, gs, ge, gn = [A * g for g in pressure_ghosts(t)]
        wsend[t, 0, :levels] = pre[0, :levels] + gw
        wsend[t, 0, levels:] = pre[0, levels:] + corner(gs, gn, 0)
        wsend[t, 1, :levels] = pre[1, :levels] + corner(gw, ge, 0)
        wsend[t, 1, levels:] = pre[1, levels:] + gs
        wsend[t, 2, :levels] = pre[2, :levels] - ge
        wsend[t, 2, levels:] = pre[2, levels:] + corner(gs, gn, last)
        wsend[t, 3, :levels] = pre[3, :levels] + corner(gw, ge, last)
        wsend[t, 3, levels:] = pre[3, levels:] - gn
        for s in range(4):
            w_copy(t, s).start()

        we[:, 0, :] = we[:, 0, :] + gw
        we[:, last, :] = we[:, last, :] - ge
        terms = lane_terms(gs, -gn)
        for j in range(levels):
            wn[j] = wn[j] + terms[j]

        @pl.when(has_above)
        def _():
            up_copy(t).wait_send()
            down_copy(t).wait_recv()
            wu[levels - 1] = wu[levels - 1] - B * (above[t] - p[levels - 1])

        @pl.when(jnp.logical_not(has_above))
        def _():
            wu[levels - 1] = jnp.zeros((tile, tile), jnp.float32)

        @pl.when(has_below & (t == 0))
        def _():
            wub_copy().wait_recv()

        @pl.when(has_below)
        def _():
            down_copy(t).wait_send()
            up_copy(t).wait_recv()
            wu_below[...] = wu_below[...] - B * (p[0] - below[t])

        for j in range(levels):
            under = wu_below[...] if j == 0 else wu[j - 1]
            p[j] = p[j] - st[j] * (A * (d_rows(we[j]) + d_lanes(wn[j])) + B * (wu[j] - under))
        south, north = columns([p[j] for j in range(levels)])
        pre[0, :levels] = p[:, 0, :]
        pre[1, :levels] = south
        pre[2, :levels] = p[:, last, :]
        pre[3, :levels] = north

        gw, gs, ge, gn = wind_ghosts(t)

        @pl.when(t < SUBSTEPS - 1)
        def _():
            psend[t + 1, 0] = pre[0, :levels] + st_rims[0] * (gw + corner(gs, gn, 0))
            psend[t + 1, 1] = pre[1, :levels] + st_rims[1] * (gs + corner(gw, ge, 0))
            psend[t + 1, 2] = pre[2, :levels] + st_rims[2] * (corner(gs, gn, last) - ge)
            psend[t + 1, 3] = pre[3, :levels] + st_rims[3] * (corner(gw, ge, last) - gn)
            for s in range(4):
                p_copy(t + 1, s).start()

        p[:, 0, :] = p[:, 0, :] + st_rims[0] * gw
        p[:, last, :] = p[:, last, :] - st_rims[2] * ge
        terms = lane_terms(st_rims[1] * gs, -(st_rims[3] * gn))
        for j in range(levels):
            p[j] = p[j] + terms[j]
        return carry

    lax.fori_loop(0, SUBSTEPS, substep, 0)

    def drain(t, carry):
        for s in range(4):
            p_copy(t, s).wait_send()
            w_copy(t, s).wait_send()
        return carry

    lax.fori_loop(0, SUBSTEPS, drain, 0)

    @pl.when(has_above)
    def _():
        wub_copy().wait_send()


def run_substeps(sizes, pressure, wind_east, wind_north, wind_up, stiffness, edge_table):
    levels, tile, _ = pressure.shape
    field = jax.ShapeDtypeStruct(pressure.shape, jnp.float32)
    in_vmem = pl.BlockSpec(memory_space=pltpu.VMEM)
    n = SUBSTEPS
    return pl.pallas_call(
        functools.partial(substeps_kernel, sizes),
        out_shape=[field] * 4,
        in_specs=[pl.BlockSpec(memory_space=pltpu.SMEM)] + [in_vmem] * 5,
        out_specs=[in_vmem] * 4,
        scratch_shapes=[
            pltpu.VMEM((n, 4, levels, tile), jnp.float32),
            pltpu.VMEM((n, 4, 4, levels, tile), jnp.float32),
            pltpu.VMEM((n, 4, 2 * levels, tile), jnp.float32),
            pltpu.VMEM((n, 4, 4, 2 * levels, tile), jnp.float32),
            pltpu.VMEM((n, tile, tile), jnp.float32),
            pltpu.VMEM((n, tile, tile), jnp.float32),
            pltpu.VMEM((tile, tile), jnp.float32),
            pltpu.VMEM((tile, tile), jnp.float32),
            pltpu.VMEM((tile, tile), jnp.float32),
            pltpu.VMEM((4, 2 * levels, tile), jnp.float32),
            pltpu.VMEM((4, levels, tile), jnp.float32),
            pltpu.SemaphoreType.DMA((n, 4)),
            pltpu.SemaphoreType.DMA((n, 4)),
            pltpu.SemaphoreType.DMA((n, 4)),
            pltpu.SemaphoreType.DMA((n, 4)),
            pltpu.SemaphoreType.DMA((2, n)),
            pltpu.SemaphoreType.DMA((2, n)),
            pltpu.SemaphoreType.DMA((2,)),
        ],
        compiler_params=pltpu.CompilerParams(
            collective_id=0, has_side_effects=True, vmem_limit_bytes=32 * 2**20
        ),
    )(edge_table, pressure, wind_east, wind_north, wind_up, stiffness)


def slots_kernel(owner_count, slot_count, owner, source, weight, slot_source, slot_weight):
    rows = owner.shape[0]
    slot_rows = slot_source.shape[0]
    names = owner[...]
    up_to = (iota((LANES, LANES), 0) <= iota((LANES, LANES), 1)).astype(jnp.bfloat16)
    ones = jnp.ones((LANES, LANES), jnp.bfloat16)
    before = (iota((rows, rows), 0) > iota((rows, rows), 1)).astype(jnp.bfloat16)

    def count(o, rank):
        named = names == o
        hot = named.astype(jnp.float32).astype(jnp.bfloat16)
        within = jnp.dot(hot, up_to, preferred_element_type=jnp.float32)
        total = jnp.dot(hot, ones, preferred_element_type=jnp.float32).astype(jnp.bfloat16)
        earlier = jnp.dot(before, total, preferred_element_type=jnp.float32)
        return jnp.where(named, within + earlier - 1.0, rank)

    rank = lax.fori_loop(0, owner_count, count, jnp.zeros(names.shape, jnp.float32))
    slot = names * slot_count + rank.astype(jnp.int32)
    slot_high, slot_low = slot >> 7, slot & (LANES - 1)
    src = source[...]
    w = weight[...]
    w1 = w.astype(jnp.bfloat16).astype(jnp.float32)
    w2 = (w - w1).astype(jnp.bfloat16).astype(jnp.float32)
    w3 = w - w1 - w2
    pieces = [(src >> 7).astype(jnp.float32), (src & (LANES - 1)).astype(jnp.float32), w1, w2, w3]
    high_place, low_place = iota((slot_rows, LANES), 0), iota((LANES, LANES), 0)
    total = jnp.zeros((len(pieces) * slot_rows, LANES), jnp.float32)
    for r in range(rows):
        here = high_place == slot_high[r : r + 1]
        left = jnp.concatenate([jnp.where(here, piece[r : r + 1], 0.0) for piece in pieces], axis=0)
        right = jnp.where(low_place == slot_low[r : r + 1], 1.0, 0.0)
        total += dot_nt(left.astype(jnp.bfloat16), right.astype(jnp.bfloat16))
    part = [total[k * slot_rows : (k + 1) * slot_rows] for k in range(len(pieces))]
    slot_source[...] = (part[0] * LANES + part[1]).astype(jnp.int32)
    slot_weight[...] = part[2] + part[3] + part[4]


def take_kernel(p, we, wn, wu, slot_source, slot_weight, payload, high, low):
    levels, tile, _ = p.shape
    half = tile // 2
    for q, field in enumerate((p, we, wn, wu)):
        for l in range(levels):
            h, d = parts2(field[l].T)
            at = pl.ds((q * levels + l) * half, half)
            high[at, :tile], high[at, tile:] = h[:half], h[half:]
            low[at, :tile], low[at, tile:] = d[:half], d[half:]
    count = 4 * levels

    def step(b, carry):
        src = jnp.concatenate([slot_source[pl.ds(2 * b, 1), :], slot_source[pl.ds(2 * b + 1, 1), :]], axis=1)
        w = jnp.concatenate([slot_weight[pl.ds(2 * b, 1), :], slot_weight[pl.ds(2 * b + 1, 1), :]], axis=1)
        x, y = src >> 7, src & (tile - 1)
        line = x + jnp.where(y >= half, tile, 0)
        hot = jnp.where(iota((2 * tile, BLOCK), 0) == line, 1.0, 0.0).astype(jnp.bfloat16)
        picked = jnp.dot(high[...], hot, preferred_element_type=jnp.float32)
        picked += jnp.dot(low[...], hot, preferred_element_type=jnp.float32)
        mask = jnp.where(iota((half, BLOCK), 0) == (y & (half - 1)), w, 0.0)
        payload[:, pl.ds(pl.multiple_of(b * BLOCK, BLOCK), BLOCK)] = jnp.sum(
            picked.reshape(count, half, BLOCK) * mask[None], axis=1
        )
        return carry

    lax.fori_loop(0, payload.shape[1] // BLOCK, step, 0)


def land_kernel(arrived, cell, out, total):
    count = arrived.shape[0]
    groups = out.shape[1] // BLOCK
    total[...] = jnp.zeros(total.shape, jnp.float32)

    def step(b, carry):
        c = jnp.concatenate([cell[pl.ds(2 * b, 1), :], cell[pl.ds(2 * b + 1, 1), :]], axis=1)
        values = arrived[:, pl.ds(pl.multiple_of(b * BLOCK, BLOCK), BLOCK)]
        h = values.astype(jnp.bfloat16).astype(jnp.float32)
        group = c >> 8
        spread = [jnp.where(group == g, h, 0.0) for g in range(groups)]
        spread += [jnp.where(group == g, values - h, 0.0) for g in range(groups)]
        hot = jnp.where(iota((BLOCK, BLOCK), 0) == (c & (BLOCK - 1)), 1.0, 0.0)
        total[...] += dot_nt(jnp.concatenate(spread, axis=0).astype(jnp.bfloat16), hot.astype(jnp.bfloat16))
        return carry

    lax.fori_loop(0, arrived.shape[1] // BLOCK, step, 0)
    for g in range(groups):
        out[:, g * BLOCK : (g + 1) * BLOCK] = (
            total[g * count : (g + 1) * count] + total[(groups + g) * count : (groups + g + 1) * count]
        )


def local_call(kernel, out_shape, scratch=()):
    return pl.pallas_call(
        kernel,
        out_shape=out_shape,
        scratch_shapes=list(scratch),
        compiler_params=pltpu.CompilerParams(vmem_limit_bytes=40 * 2**20),
    )


def per_device(
    sizes,
    pressure,
    wind_east,
    wind_north,
    wind_up,
    stiffness,
    edge_table,
    remap_source,
    remap_weight,
    remap_owner,
    latlon_cell,
):
    levels, tile, _ = pressure.shape
    owner_count = sizes[0]
    slots = latlon_cell.shape[0]
    slot_count = slots // owner_count
    cell_count = tile * tile // 8
    count = 4 * levels
    f32 = jnp.float32
    slot_source, slot_weight = local_call(
        functools.partial(slots_kernel, owner_count, slot_count),
        [
            jax.ShapeDtypeStruct((slots // LANES, LANES), jnp.int32),
            jax.ShapeDtypeStruct((slots // LANES, LANES), f32),
        ],
    )(
        remap_owner.reshape(-1, LANES),
        remap_source.reshape(-1, LANES),
        remap_weight.reshape(-1, LANES),
    )
    fields = run_substeps(sizes, pressure, wind_east, wind_north, wind_up, stiffness, edge_table)
    payload = local_call(
        take_kernel,
        jax.ShapeDtypeStruct((count, slots), f32),
        [pltpu.VMEM((count * tile // 2, 2 * tile), jnp.bfloat16)] * 2,
    )(*fields, slot_source, slot_weight)
    arrived = lax.all_to_all(payload, "px", split_axis=1, concat_axis=1, tiled=True)
    groups = cell_count // BLOCK
    latlon = local_call(
        land_kernel,
        jax.ShapeDtypeStruct((count, cell_count), f32),
        [pltpu.VMEM((2 * groups * count, BLOCK), f32)],
    )(arrived, latlon_cell.reshape(-1, LANES))
    return fields[0], latlon.reshape(4, levels, cell_count)


def solution(mesh):
    field = P("lev", "px", "py")
    entries = P(("px", "py"))
    sizes = (mesh.shape["px"], mesh.shape["py"], mesh.shape["lev"])
    return jax.shard_map(
        functools.partial(per_device, sizes),
        mesh=mesh,
        in_specs=(field,) * 5 + (P(), entries, entries, P(("px", "py"), None), entries),
        out_specs=(field, P(None, "lev", ("px", "py"))),
        check_vma=False,
    )
```

time: 241 us -> 89.7 us (0.37)
  other arithmetic: 92.2 us -> 0 us
  starting transfers between devices: 62.4 us -> 0 us
  Pallas kernels: 0 us -> 62.1 us
  waiting for transfers between devices: 44.8 us -> 0 us
  local copies, waits for them, and re-layouts: 28 us -> 9.08 us
  blocking collectives: 0 us -> 17.3 us
  between operations: 12.5 us -> 0.7 us
    pallas_call x0 -> x4, Pallas kernels: none -> 62.1 us  [the longest x1 37.9 us: run_substeps(): pl.pallas_call(functools.partial(substeps_kernel, sizes), out_shape=[fiel...]
    ppermute x40 -> x0, starting transfers between devices: 58.9 us -> none  [the longest x8 23.1 us: shifted(): return lax.ppermute(shard, axis, pairs)]
    scatter-add x1 -> x0, other arithmetic: 44.6 us -> none  [per_device(): jnp.zeros((4 * levels, cell_count), jnp.float32).at[:, latlon_cell]]
    scatter x1 -> x0, other arithmetic: 37.8 us -> none  [per_device(): jnp.zeros((4 * levels, owner_count * slot_count), jnp.float32)]
    ppermute x40 -> x0, waiting for transfers between devices: 31.4 us -> none  [the longest x16 20 us: extended_2(): lax.ppermute(tail, axis, [(i, (i + 1) % count) for i in range(count)])]
    all_to_all x0 -> x1, blocking collectives: none -> 17.3 us  [per_device(): lax.all_to_all(payload, 'px', split_axis=1, concat_axis=1, tiled=True)]
    all_to_all x1 -> x0, waiting for transfers between devices: 13.5 us -> none  [per_device(): lax.all_to_all(outgoing, 'px', split_axis=1, concat_axis=1, tiled=True)]
    slice x56 -> x0, local copies, waits for them, and re-layouts: 8.52 us -> none  [the longest x4 2.3 us: rim_stack(): south_rim = fields[:, :, :, 0]]
  transfers between devices with their start and end apart: 41 -> 0, of which waited for: 23 -> 0; matrix products, arithmetic and copies ran while one was open for 9% -> 0% of each run, Pallas kernels for 0% -> 0%
where the time goes in v1:
time: 89.7 us; the launch traced here: 89.2 us
  Pallas kernels  62.1 us (69%)
  blocking collectives  17.3 us (19%)
  local copies, waits for them, and re-layouts  9.08 us (10%)
    pallas_call x1, Pallas kernels, run_substeps(): pl.pallas_call(functools.partial(substeps_kernel, sizes), out_shape=[fiel...  37.9 us
    all_to_all x1, blocking collectives, per_device(): lax.all_to_all(payload, 'px', split_axis=1, concat_axis=1, tiled=True)  17.3 us
    pallas_call x1, Pallas kernels, per_device(): local_call(take_kernel, jax.ShapeDtypeStruct((count, slots), f32), [pltpu...  14.8 us
    unnamed x21, local copies, waits for them, and re-layouts  8.31 us
    pallas_call x1, Pallas kernels, per_device(): local_call(land_kernel, jax.ShapeDtypeStruct((count, cell_count), f32), [...  7.51 us
    pallas_call x1, Pallas kernels, per_device(): local_call(functools.partial(slots_kernel, owner_count, slot_count), [jax...  1.94 us

profile of v1, /device:TPU:0, one launch (start us, length us, event | category | flops | bytes accessed | tf_op | source)
XLA Modules:
  0.0 89.2 jit_solution(17081945862596508944)
XLA Ops:
  0.6 0.0 copy-start.6
  0.6 0.7 copy-done.6
  1.3 0.0 copy-start.7
  1.4 0.7 copy-done.7
  2.1 0.0 copy-start.8
  2.1 0.7 copy-done.8
  2.8 0.0 copy-start.9
  2.8 1.9 %shard_map.114 = (s32[64,128]{1,0:T(8,128)S(1)}, f32[64,128]{1,0:T(8,128)S(1)}) custom-call(s32[32,128]{1,0:T(8,128)S(1)} %bitcast.13, s32[32,128]{1,0:T(8,128)S(1)} %bitcast.14, f32[32,128]{1,0:T(8,128)S(1)} %bitcast.15), custom_call_target="tpu_custom_call" | custom-call | tf_op jit(solution)/shard_map/pallas_call | solution.py:490
  4.7 0.0 copy-done.9
  4.7 0.0 copy-start
  4.7 0.9 %copy-done = f32[4,128,128]{2,1,0:T(8,128)S(1)} copy-done((f32[4,128,128]{2,1,0:T(8,128)S(1)}, f32[4,128,128]{2,1,0:T(8,128)}, u32[]{:S(2)}) %copy-start) | copy-done | bytes 262168
  5.7 0.0 copy-start.1
  5.7 0.9 %copy-done.1 = f32[4,128,128]{2,1,0:T(8,128)S(1)} copy-done((f32[4,128,128]{2,1,0:T(8,128)S(1)}, f32[4,128,128]{2,1,0:T(8,128)}, u32[]{:S(2)}) %copy-start.1) | copy-done | bytes 262168
  6.6 0.0 copy-start.2
  6.6 0.9 %copy-done.2 = f32[4,128,128]{2,1,0:T(8,128)S(1)} copy-done((f32[4,128,128]{2,1,0:T(8,128)S(1)}, f32[4,128,128]{2,1,0:T(8,128)}, u32[]{:S(2)}) %copy-start.2) | copy-done | bytes 262168
  7.6 0.0 copy-start.3
  7.6 0.9 %copy-done.3 = f32[4,128,128]{2,1,0:T(8,128)S(1)} copy-done((f32[4,128,128]{2,1,0:T(8,128)S(1)}, f32[4,128,128]{2,1,0:T(8,128)}, u32[]{:S(2)}) %copy-start.3) | copy-done | bytes 262168
  8.5 0.0 copy-start.4
  8.5 0.9 %copy-done.4 = f32[4,128,128]{2,1,0:T(8,128)S(1)} copy-done((f32[4,128,128]{2,1,0:T(8,128)S(1)}, f32[4,128,128]{2,1,0:T(8,128)}, u32[]{:S(2)}) %copy-start.4) | copy-done | bytes 262168
  9.5 37.9 %shard_map.113 = (f32[4,128,128]{2,1,0:T(8,128)S(1)}, f32[4,128,128]{2,1,0:T(8,128)S(1)}, f32[4,128,128]{2,1,0:T(8,128)S(1)}, f32[4,128,128]{2,1,0:T(8,128)S(1)}) custom-call(s32[4,4,4]{2,1,0:T(4,128)S(1)} %copy-done.9, f32[4,128,128]{2,1,0:T(8,128)S(1)} %copy-done, f32[4,128,128]{2,1,0:T(8,128)S(1)} %copy-done.1, f32[4,128,128]{2,1,0:T(8,128)S(1)} %copy-done.2, ...), custom_call_target="tpu_custom_call" | custom-call | tf_op jit(solution)/shard_map/pallas_call | solution.py:342
  47.4 14.8 %shard_map.115 = f32[16,8192]{1,0:T(8,128)S(1)} custom-call(f32[4,128,128]{2,1,0:T(8,128)S(1)} %get-tuple-element.16.p, f32[4,128,128]{2,1,0:T(8,128)S(1)} %get-tuple-element.9.we, f32[4,128,128]{2,1,0:T(8,128)S(1)} %get-tuple-element.10.wn, f32[4,128,128]{2,1,0:T(8,128)S(1)} %get-tuple-element.11.wu, s32[64,128]{1,0:T(8,128)S(1)} %get-tuple-element.12.slot_source, ...), custom_call_target="tpu_custom_call" | custom-call | tf_op jit(solution)/shard_map/pallas_call | solution.py:502
  62.2 17.3 %all_to_all.11 = f32[16,4,2048]{2,0,1:T(8,128)S(1)} all-to-all(f32[16,4,2048]{2,0,1:T(8,128)S(1)} %bitcast.16), channel_id=1, replica_groups=mesh['px'=4,'py'=4,'lev'=2] {'px'}, dimensions={1} | all-to-all | bytes 1048576 | tf_op jit(solution)/shard_map/all_to_all | solution.py:507
  79.5 0.0 copy-start.5
  79.5 0.7 copy-done.5
  80.3 7.5 %shard_map.116 = f32[16,2048]{1,0:T(8,128)S(1)} custom-call(f32[16,8192]{1,0:T(8,128)S(1)} %bitcast.11, s32[64,128]{1,0:T(8,128)S(1)} %bitcast.12), custom_call_target="tpu_custom_call" | custom-call | tf_op jit(solution)/shard_map/pallas_call | solution.py:509
  87.8 0.7 reshape.25
  88.5 0.7 copy.19
  (2 shorter events, 0.1 us)
Async XLA Ops:
  0.6 0.7 copy-start.6
  1.3 0.7 copy-start.7
  2.1 0.7 copy-start.8
  2.8 1.9 %copy-start.9 = (s32[4,4,4]{2,1,0:T(4,128)S(1)}, s32[4,4,4]{2,1,0:T(4,128)}, u32[]{:S(2)}) copy-start(s32[4,4,4]{2,1,0:T(4,128)} %edges.1) | copy-start | bytes 772
  4.7 1.0 %copy-start = (f32[4,128,128]{2,1,0:T(8,128)S(1)}, f32[4,128,128]{2,1,0:T(8,128)}, u32[]{:S(2)}) copy-start(f32[4,128,128]{2,1,0:T(8,128)} %p_in.1) | copy-start | bytes 786436
  5.7 0.9 %copy-start.1 = (f32[4,128,128]{2,1,0:T(8,128)S(1)}, f32[4,128,128]{2,1,0:T(8,128)}, u32[]{:S(2)}) copy-start(f32[4,128,128]{2,1,0:T(8,128)} %we_in.1) | copy-start | bytes 786436
  6.6 0.9 %copy-start.2 = (f32[4,128,128]{2,1,0:T(8,128)S(1)}, f32[4,128,128]{2,1,0:T(8,128)}, u32[]{:S(2)}) copy-start(f32[4,128,128]{2,1,0:T(8,128)} %wn_in.1) | copy-start | bytes 786436
  7.6 0.9 %copy-start.3 = (f32[4,128,128]{2,1,0:T(8,128)S(1)}, f32[4,128,128]{2,1,0:T(8,128)}, u32[]{:S(2)}) copy-start(f32[4,128,128]{2,1,0:T(8,128)} %wu_in.1) | copy-start | bytes 786436
  8.5 0.9 %copy-start.4 = (f32[4,128,128]{2,1,0:T(8,128)S(1)}, f32[4,128,128]{2,1,0:T(8,128)}, u32[]{:S(2)}) copy-start(f32[4,128,128]{2,1,0:T(8,128)} %st.1) | copy-start | bytes 786436
  79.5 0.8 copy-start.5

commit v2 on v1

--- a/solution.py
+++ b/solution.py
@@ -28,18 +28,28 @@
     return lax.dot_general(a, b, (((1,), (1,)), ((), ())), preferred_element_type=jnp.float32)
 
 
-def substeps_kernel(
+def whole_kernel(
     sizes,
     edges,
     p_in,
     we_in,
     wn_in,
     wu_in,
-    st,
+    st_in,
+    owner_in,
+    source_in,
+    weight_in,
+    cell_in,
     p,
+    latlon,
     we,
     wn,
     wu,
+    st,
+    owner,
+    source,
+    weight,
+    cell,
     psend,
     precv,
     wsend,
@@ -51,6 +61,13 @@
     ghost_rows,
     pre,
     st_rims,
+    slot_source,
+    slot_weight,
+    split,
+    payload,
+    arrived,
+    total,
+    in_sems,
     psend_sem,
     precv_sem,
     wsend_sem,
@@ -58,10 +75,30 @@
     up_sems,
     down_sems,
     wub_sems,
+    give_sem,
+    take_sem,
 ):
     n_px, n_py, n_lev = sizes
-    levels, tile, _ = p_in.shape
+    levels, tile, _ = p.shape
     last = tile - 1
+    loads = [
+        pltpu.make_async_copy(src, dst, in_sems.at[k])
+        for k, (src, dst) in enumerate(
+            (
+                (p_in, p),
+                (wu_in, wu),
+                (owner_in, owner),
+                (source_in, source),
+                (weight_in, weight),
+                (st_in, st),
+                (we_in, we),
+                (wn_in, wn),
+                (cell_in, cell),
+            )
+        )
+    ]
+    for load in loads:
+        load.start()
     ix, iy, iz = lax.axis_index("px"), lax.axis_index("py"), lax.axis_index("lev")
     targets = (
         {"px": lax.rem(ix + 1, n_px)},
@@ -72,8 +109,14 @@
     has_above, has_below = iz < n_lev - 1, iz > 0
 
     barrier = pltpu.get_barrier_semaphore()
-    for target in targets:
+    for target in (targets[1], targets[3]):
         pl.semaphore_signal(barrier, inc=1, device_id=target, device_id_type=MESH)
+
+    def greet(d, carry):
+        pl.semaphore_signal(barrier, inc=1, device_id={"px": lax.rem(ix + d, n_px)}, device_id_type=MESH)
+        return carry
+
+    lax.fori_loop(1, n_px, greet, 0)
 
     @pl.when(has_above)
     def _():
@@ -118,7 +161,7 @@
 
     def wub_copy():
         return pltpu.make_async_remote_copy(
-            src_ref=wu_in.at[levels - 1],
+            src_ref=wu.at[levels - 1],
             dst_ref=wu_below,
             send_sem=wub_sems.at[0],
             recv_sem=wub_sems.at[1],
@@ -203,16 +246,37 @@
             return jnp.where(first_lane, first, 0.0) - jnp.where(last_lane, pltpu.roll(second, last, 1), 0.0)
         return jnp.where(first_lane, pltpu.roll(first, 1, 1), 0.0) - jnp.where(last_lane, second, 0.0)
 
-    p[...] = p_in[...]
-    south, north = columns([p_in[j] for j in range(levels)])
-    psend[0, 0] = p_in[:, 0, :]
+    def give_copy(o):
+        return pltpu.make_async_remote_copy(
+            src_ref=payload.at[o],
+            dst_ref=arrived.at[ix],
+            send_sem=give_sem.at[o],
+            recv_sem=take_sem.at[ix],
+            device_id={"px": o},
+            device_id_type=MESH,
+        )
+
+    def got(o):
+        return pltpu.make_async_remote_copy(
+            src_ref=payload.at[o],
+            dst_ref=arrived.at[o],
+            send_sem=give_sem.at[o],
+            recv_sem=take_sem.at[o],
+            device_id={"px": o},
+            device_id_type=MESH,
+        )
+
+    loads[0].wait()
+    south, north = columns([p[j] for j in range(levels)])
+    psend[0, 0] = p[:, 0, :]
     psend[0, 1] = south
-    psend[0, 2] = p_in[:, last, :]
+    psend[0, 2] = p[:, last, :]
     psend[0, 3] = north
 
-    pl.semaphore_wait(barrier, 4 + has_above.astype(jnp.int32) + has_below.astype(jnp.int32))
+    pl.semaphore_wait(barrier, n_px + 1 + has_above.astype(jnp.int32) + has_below.astype(jnp.int32))
     for s in range(4):
         p_copy(0, s).start()
+    loads[1].wait()
 
     @pl.when(has_above)
     def _():
@@ -222,15 +286,19 @@
     def _():
         wu_below[...] = jnp.zeros((tile, tile), jnp.float32)
 
+    for load in loads[2:]:
+        load.wait()
     ghost_rows[...] = jnp.zeros((tile, tile), jnp.float32)
     south, north = columns([st[j] for j in range(levels)])
     st_rims[0] = st[:, 0, :] * A
     st_rims[1] = south * A
     st_rims[2] = st[:, last, :] * A
     st_rims[3] = north * A
-    we[...] = we_in[...]
-    wn[...] = wn_in[...]
-    wu[...] = wu_in[...]
+    slot_count = payload.shape[2]
+    find_slots(n_px, slot_count, owner, source, weight, slot_source, slot_weight)
+
+    def ahead(d):
+        return lax.rem(ix + d + 1, n_px)
 
     def substep(t, carry):
         @pl.when(has_above)
@@ -272,6 +340,10 @@
         for j in range(levels):
             wn[j] = wn[j] + terms[j]
 
+        @pl.when(has_above & (t == 0))
+        def _():
+            wub_copy().wait_send()
+
         @pl.when(has_above)
         def _():
             up_copy(t).wait_send()
@@ -301,6 +373,12 @@
         pre[2, :levels] = p[:, last, :]
         pre[3, :levels] = north
 
+        @pl.when(t == SUBSTEPS - 1)
+        def _():
+            for q, field in ((1, we), (2, wn), (3, wu)):
+                split_field(split, field, q)
+            pick(split, slot_source, slot_weight, payload, ahead(0), ahead(0), 1, 4)
+
         gw, gs, ge, gn = wind_ghosts(t)
 
         @pl.when(t < SUBSTEPS - 1)
@@ -321,6 +399,33 @@
 
     lax.fori_loop(0, SUBSTEPS, substep, 0)
 
+    split_field(split, p, 0)
+    pick(split, slot_source, slot_weight, payload, ahead(0), ahead(0), 0, 1)
+    give_copy(ahead(0)).start()
+
+    def hand_out(d, carry):
+        pick(split, slot_source, slot_weight, payload, ahead(d), ahead(d), 0, 4)
+        give_copy(ahead(d)).start()
+        return carry
+
+    lax.fori_loop(1, n_px - 1, hand_out, 0)
+    pick(split, slot_source, slot_weight, arrived, ix, ix, 0, 4)
+    total[...] = jnp.zeros(total.shape, jnp.float32)
+    land(arrived, cell, ix, total)
+
+    def bring_in(d, carry):
+        o = lax.rem(ix + n_px - d - 1, n_px)
+        got(o).wait_recv()
+        land(arrived, cell, o, total)
+        return carry
+
+    lax.fori_loop(0, n_px - 1, bring_in, 0)
+    count, groups = 4 * levels, latlon.shape[2] // BLOCK
+    for g in range(groups):
+        both = total[g * count : (g + 1) * count] + total[(groups + g) * count : (groups + g + 1) * count]
+        for q in range(4):
+            latlon[q, :, g * BLOCK : (g + 1) * BLOCK] = both[q * levels : (q + 1) * levels]
+
     def drain(t, carry):
         for s in range(4):
             p_copy(t, s).wait_send()
@@ -329,48 +434,14 @@
 
     lax.fori_loop(0, SUBSTEPS, drain, 0)
 
-    @pl.when(has_above)
-    def _():
-        wub_copy().wait_send()
-
-
-def run_substeps(sizes, pressure, wind_east, wind_north, wind_up, stiffness, edge_table):
-    levels, tile, _ = pressure.shape
-    field = jax.ShapeDtypeStruct(pressure.shape, jnp.float32)
-    in_vmem = pl.BlockSpec(memory_space=pltpu.VMEM)
-    n = SUBSTEPS
-    return pl.pallas_call(
-        functools.partial(substeps_kernel, sizes),
-        out_shape=[field] * 4,
-        in_specs=[pl.BlockSpec(memory_space=pltpu.SMEM)] + [in_vmem] * 5,
-        out_specs=[in_vmem] * 4,
-        scratch_shapes=[
-            pltpu.VMEM((n, 4, levels, tile), jnp.float32),
-            pltpu.VMEM((n, 4, 4, levels, tile), jnp.float32),
-            pltpu.VMEM((n, 4, 2 * levels, tile), jnp.float32),
-            pltpu.VMEM((n, 4, 4, 2 * levels, tile), jnp.float32),
-            pltpu.VMEM((n, tile, tile), jnp.float32),
-            pltpu.VMEM((n, tile, tile), jnp.float32),
-            pltpu.VMEM((tile, tile), jnp.float32),
-            pltpu.VMEM((tile, tile), jnp.float32),
-            pltpu.VMEM((tile, tile), jnp.float32),
-            pltpu.VMEM((4, 2 * levels, tile), jnp.float32),
-            pltpu.VMEM((4, levels, tile), jnp.float32),
-            pltpu.SemaphoreType.DMA((n, 4)),
-            pltpu.SemaphoreType.DMA((n, 4)),
-            pltpu.SemaphoreType.DMA((n, 4)),
-            pltpu.SemaphoreType.DMA((n, 4)),
-            pltpu.SemaphoreType.DMA((2, n)),
-            pltpu.SemaphoreType.DMA((2, n)),
-            pltpu.SemaphoreType.DMA((2,)),
-        ],
-        compiler_params=pltpu.CompilerParams(
-            collective_id=0, has_side_effects=True, vmem_limit_bytes=32 * 2**20
-        ),
-    )(edge_table, pressure, wind_east, wind_north, wind_up, stiffness)
-
-
-def slots_kernel(owner_count, slot_count, owner, source, weight, slot_source, slot_weight):
+    def sent(d, carry):
+        give_copy(ahead(d)).wait_send()
+        return carry
+
+    lax.fori_loop(0, n_px - 1, sent, 0)
+
+
+def find_slots(owner_count, slot_count, owner, source, weight, slot_source, slot_weight):
     rows = owner.shape[0]
     slot_rows = slot_source.shape[0]
     names = owner[...]
@@ -407,64 +478,64 @@
     slot_weight[...] = part[2] + part[3] + part[4]
 
 
-def take_kernel(p, we, wn, wu, slot_source, slot_weight, payload, high, low):
-    levels, tile, _ = p.shape
+def split_field(split, field, q):
+    levels, tile, _ = field.shape
     half = tile // 2
-    for q, field in enumerate((p, we, wn, wu)):
-        for l in range(levels):
-            h, d = parts2(field[l].T)
-            at = pl.ds((q * levels + l) * half, half)
-            high[at, :tile], high[at, tile:] = h[:half], h[half:]
-            low[at, :tile], low[at, tile:] = d[:half], d[half:]
-    count = 4 * levels
+    for l in range(levels):
+        h, d = parts2(field[l].T)
+        at = slice((q * levels + l) * half, (q * levels + l + 1) * half)
+        for k, part in enumerate((h[:half], h[half:], d[:half], d[half:])):
+            split[at, k * tile : (k + 1) * tile] = part
+
+
+def pick(split, slot_source, slot_weight, dst, place, o, first, end):
+    rows, slot_count = dst.shape[1:]
+    tile = split.shape[1] // 4
+    half = tile // 2
+    width = min(BLOCK, slot_count)
+    pieces = width // LANES
+    quarter = rows // 4
+    at = slice(first * quarter * half, end * quarter * half)
+
+    def joined(ref, b):
+        row = o * (slot_count // LANES) + b * pieces
+        return jnp.concatenate([ref[pl.ds(row + k, 1), :] for k in range(pieces)], axis=1)
 
     def step(b, carry):
-        src = jnp.concatenate([slot_source[pl.ds(2 * b, 1), :], slot_source[pl.ds(2 * b + 1, 1), :]], axis=1)
-        w = jnp.concatenate([slot_weight[pl.ds(2 * b, 1), :], slot_weight[pl.ds(2 * b + 1, 1), :]], axis=1)
+        src, w = joined(slot_source, b), joined(slot_weight, b)
         x, y = src >> 7, src & (tile - 1)
         line = x + jnp.where(y >= half, tile, 0)
-        hot = jnp.where(iota((2 * tile, BLOCK), 0) == line, 1.0, 0.0).astype(jnp.bfloat16)
-        picked = jnp.dot(high[...], hot, preferred_element_type=jnp.float32)
-        picked += jnp.dot(low[...], hot, preferred_element_type=jnp.float32)
-        mask = jnp.where(iota((half, BLOCK), 0) == (y & (half - 1)), w, 0.0)
-        payload[:, pl.ds(pl.multiple_of(b * BLOCK, BLOCK), BLOCK)] = jnp.sum(
-            picked.reshape(count, half, BLOCK) * mask[None], axis=1
-        )
-        return carry
-
-    lax.fori_loop(0, payload.shape[1] // BLOCK, step, 0)
-
-
-def land_kernel(arrived, cell, out, total):
-    count = arrived.shape[0]
-    groups = out.shape[1] // BLOCK
-    total[...] = jnp.zeros(total.shape, jnp.float32)
+        hot = jnp.where(iota((2 * tile, width), 0) == line, 1.0, 0.0).astype(jnp.bfloat16)
+        picked = jnp.dot(
+            split[at, :], jnp.concatenate([hot, hot], axis=0), preferred_element_type=jnp.float32
+        )
+        mask = jnp.where(iota((half, width), 0) == (y & (half - 1)), w, 0.0)
+        dst[place, first * quarter : end * quarter, pl.ds(pl.multiple_of(b * width, width), width)] = jnp.sum(
+            picked.reshape((end - first) * quarter, half, width) * mask[None], axis=1
+        )
+        return carry
+
+    lax.fori_loop(0, slot_count // width, step, 0)
+
+
+def land(arrived, cell, o, total):
+    count, slot_count = arrived.shape[1:]
+    groups = total.shape[0] // (2 * count)
+    width = min(4 * BLOCK, slot_count)
 
     def step(b, carry):
-        c = jnp.concatenate([cell[pl.ds(2 * b, 1), :], cell[pl.ds(2 * b + 1, 1), :]], axis=1)
-        values = arrived[:, pl.ds(pl.multiple_of(b * BLOCK, BLOCK), BLOCK)]
+        at = pl.ds(pl.multiple_of(b * width, width), width)
+        c = cell[pl.ds(o, 1), at]
+        values = arrived[o, :, at]
         h = values.astype(jnp.bfloat16).astype(jnp.float32)
         group = c >> 8
         spread = [jnp.where(group == g, h, 0.0) for g in range(groups)]
         spread += [jnp.where(group == g, values - h, 0.0) for g in range(groups)]
-        hot = jnp.where(iota((BLOCK, BLOCK), 0) == (c & (BLOCK - 1)), 1.0, 0.0)
+        hot = jnp.where(iota((BLOCK, width), 0) == (c & (BLOCK - 1)), 1.0, 0.0)
         total[...] += dot_nt(jnp.concatenate(spread, axis=0).astype(jnp.bfloat16), hot.astype(jnp.bfloat16))
         return carry
 
-    lax.fori_loop(0, arrived.shape[1] // BLOCK, step, 0)
-    for g in range(groups):
-        out[:, g * BLOCK : (g + 1) * BLOCK] = (
-            total[g * count : (g + 1) * count] + total[(groups + g) * count : (groups + g + 1) * count]
-        )
-
-
-def local_call(kernel, out_shape, scratch=()):
-    return pl.pallas_call(
-        kernel,
-        out_shape=out_shape,
-        scratch_shapes=list(scratch),
-        compiler_params=pltpu.CompilerParams(vmem_limit_bytes=40 * 2**20),
-    )
+    lax.fori_loop(0, slot_count // width, step, 0)
 
 
 def per_device(
@@ -486,32 +557,73 @@
     slot_count = slots // owner_count
     cell_count = tile * tile // 8
     count = 4 * levels
-    f32 = jnp.float32
-    slot_source, slot_weight = local_call(
-        functools.partial(slots_kernel, owner_count, slot_count),
-        [
-            jax.ShapeDtypeStruct((slots // LANES, LANES), jnp.int32),
-            jax.ShapeDtypeStruct((slots // LANES, LANES), f32),
+    rows = remap_source.shape[0] // LANES
+    f32, i32 = jnp.float32, jnp.int32
+    n = SUBSTEPS
+    field = pltpu.VMEM(pressure.shape, f32)
+    plane = pltpu.VMEM((tile, tile), f32)
+    dma = pltpu.SemaphoreType.DMA
+    in_vmem = pl.BlockSpec(memory_space=pltpu.VMEM)
+    return pl.pallas_call(
+        functools.partial(whole_kernel, sizes),
+        out_shape=[
+            jax.ShapeDtypeStruct(pressure.shape, f32),
+            jax.ShapeDtypeStruct((4, levels, cell_count), f32),
         ],
+        in_specs=[pl.BlockSpec(memory_space=pltpu.SMEM)] + [pl.BlockSpec(memory_space=pl.ANY)] * 9,
+        out_specs=[in_vmem] * 2,
+        scratch_shapes=[
+            field,
+            field,
+            field,
+            field,
+            pltpu.VMEM((rows, LANES), i32),
+            pltpu.VMEM((rows, LANES), i32),
+            pltpu.VMEM((rows, LANES), f32),
+            pltpu.VMEM((owner_count, slot_count), i32),
+            pltpu.VMEM((n, 4, levels, tile), f32),
+            pltpu.VMEM((n, 4, 4, levels, tile), f32),
+            pltpu.VMEM((n, 4, 2 * levels, tile), f32),
+            pltpu.VMEM((n, 4, 4, 2 * levels, tile), f32),
+            pltpu.VMEM((n, tile, tile), f32),
+            pltpu.VMEM((n, tile, tile), f32),
+            plane,
+            plane,
+            plane,
+            pltpu.VMEM((4, 2 * levels, tile), f32),
+            pltpu.VMEM((4, levels, tile), f32),
+            pltpu.VMEM((slots // LANES, LANES), i32),
+            pltpu.VMEM((slots // LANES, LANES), f32),
+            pltpu.VMEM((count * tile // 2, 4 * tile), jnp.bfloat16),
+            pltpu.VMEM((owner_count, count, slot_count), f32),
+            pltpu.VMEM((owner_count, count, slot_count), f32),
+            pltpu.VMEM((2 * count * (cell_count // BLOCK), BLOCK), f32),
+            dma((9,)),
+            dma((n, 4)),
+            dma((n, 4)),
+            dma((n, 4)),
+            dma((n, 4)),
+            dma((2, n)),
+            dma((2, n)),
+            dma((2,)),
+            dma((owner_count,)),
+            dma((owner_count,)),
+        ],
+        compiler_params=pltpu.CompilerParams(
+            collective_id=0, has_side_effects=True, vmem_limit_bytes=60 * 2**20
+        ),
     )(
-        remap_owner.reshape(-1, LANES),
-        remap_source.reshape(-1, LANES),
-        remap_weight.reshape(-1, LANES),
+        edge_table,
+        pressure,
+        wind_east,
+        wind_north,
+        wind_up,
+        stiffness,
+        remap_owner.reshape(rows, LANES),
+        remap_source.reshape(rows, LANES),
+        remap_weight.reshape(rows, LANES),
+        latlon_cell.reshape(owner_count, slot_count),
     )
-    fields = run_substeps(sizes, pressure, wind_east, wind_north, wind_up, stiffness, edge_table)
-    payload = local_call(
-        take_kernel,
-        jax.ShapeDtypeStruct((count, slots), f32),
-        [pltpu.VMEM((count * tile // 2, 2 * tile), jnp.bfloat16)] * 2,
-    )(*fields, slot_source, slot_weight)
-    arrived = lax.all_to_all(payload, "px", split_axis=1, concat_axis=1, tiled=True)
-    groups = cell_count // BLOCK
-    latlon = local_call(
-        land_kernel,
-        jax.ShapeDtypeStruct((count, cell_count), f32),
-        [pltpu.VMEM((2 * groups * count, BLOCK), f32)],
-    )(arrived, latlon_cell.reshape(-1, LANES))
-    return fields[0], latlon.reshape(4, levels, cell_count)
 
 
 def solution(mesh):

time: 89.7 us -> 59.8 us (0.67)
  blocking collectives: 17.3 us -> 0 us
  Pallas kernels: 62.1 us -> 55.1 us
  local copies, waits for them, and re-layouts: 9.08 us -> 3.75 us
    all_to_all x1 -> x0, blocking collectives: 17.3 us -> none  [per_device(): lax.all_to_all(payload, 'px', split_axis=1, concat_axis=1, tiled=True)]
    pallas_call x4 -> x1, Pallas kernels: 62.1 us -> 55.1 us  [per_device(): pl.pallas_call(functools.partial(whole_kernel, sizes), out_shape=[jax.Sha...]
    unnamed x21 -> x4, local copies, waits for them, and re-layouts: 8.31 us -> 2.36 us
where the time goes in v2:
time: 59.8 us; the launch traced here: 59.5 us
  Pallas kernels  55.1 us (92%)
  local copies, waits for them, and re-layouts  3.75 us (6%)
  between operations  0.65 us (1%)
    pallas_call x1, Pallas kernels, per_device(): pl.pallas_call(functools.partial(whole_kernel, sizes), out_shape=[jax.Sha...  55.1 us
    unnamed x4, local copies, waits for them, and re-layouts  2.36 us
    reshape x1, local copies, waits for them, and re-layouts, per_device(): latlon_cell.reshape(owner_count, slot_count)  1.39 us

profile of v2, /device:TPU:0, one launch (start us, length us, event | category | flops | bytes accessed | tf_op | source)
XLA Modules:
  0.0 59.5 jit_solution(11450790257686320275)
XLA Ops:
  0.6 1.4 %reshape.19.cell_in = s32[4,2048]{1,0:T(4,128)} reshape(s32[8192]{0:T(1024)} %param.19) | data formatting | bytes 65536 | tf_op jit(solution)/shard_map/reshape | solution.py:625
  2.0 55.1 %shard_map.113 = (f32[4,128,128]{2,1,0:T(8,128)}, f32[4,4,2048]{2,1,0:T(4,128)}) custom-call(s32[4,4,4]{2,1,0:T(4,128)} %edges.1, f32[4,128,128]{2,1,0:T(8,128)} %p_in.1, f32[4,128,128]{2,1,0:T(8,128)} %we_in.1, f32[4,128,128]{2,1,0:T(8,128)} %wn_in.1, f32[4,128,128]{2,1,0:T(8,128)} %wu_in.1, f32[4,128,128]{2,1,0:T(8,128)} %st_in.1, s32[32,128]{1,0:T(8,128)} %bitcast.3, ...), custom_call_target="tpu_custom_call" | custom-call | tf_op jit(solution)/shard_map/pallas_call | solution.py:567
  57.1 0.0 copy-start
  57.1 1.7 %copy.14 = f32[4,128,128]{2,1,0:T(8,128)} copy(f32[4,128,128]{2,1,0:T(8,128)} %get-tuple-element.4) | data formatting | bytes 524288
  58.8 0.0 copy-done
  58.8 0.7 %copy.15 = f32[4,4,2048]{2,1,0:T(4,128)} copy(f32[4,4,2048]{2,1,0:T(4,128)S(1)} %copy-done) | data formatting | bytes 262144
Async XLA Ops:
  57.1 1.7 %copy-start = (f32[4,4,2048]{2,1,0:T(4,128)S(1)}, f32[4,4,2048]{2,1,0:T(4,128)}, u32[]{:S(2)}) copy-start(f32[4,4,2048]{2,1,0:T(4,128)} %get-tuple-element.5) | copy-start | bytes 393220

commit v3 on v2

--- a/solution.py
+++ b/solution.py
@@ -246,25 +246,35 @@
             return jnp.where(first_lane, first, 0.0) - jnp.where(last_lane, pltpu.roll(second, last, 1), 0.0)
         return jnp.where(first_lane, pltpu.roll(first, 1, 1), 0.0) - jnp.where(last_lane, second, 0.0)
 
-    def give_copy(o):
+    def give_copy(o, k):
+        part = (pl.ds(0, 3), pl.ds(3, 1))[k]
         return pltpu.make_async_remote_copy(
-            src_ref=payload.at[o],
-            dst_ref=arrived.at[ix],
-            send_sem=give_sem.at[o],
-            recv_sem=take_sem.at[ix],
+            src_ref=payload.at[o, part],
+            dst_ref=arrived.at[ix, part],
+            send_sem=give_sem.at[k, o],
+            recv_sem=take_sem.at[k, ix],
             device_id={"px": o},
             device_id_type=MESH,
         )
 
-    def got(o):
+    def got(o, k):
+        part = (pl.ds(0, 3), pl.ds(3, 1))[k]
         return pltpu.make_async_remote_copy(
-            src_ref=payload.at[o],
-            dst_ref=arrived.at[o],
-            send_sem=give_sem.at[o],
-            recv_sem=take_sem.at[o],
+            src_ref=payload.at[o, part],
+            dst_ref=arrived.at[o, part],
+            send_sem=give_sem.at[k, o],
+            recv_sem=take_sem.at[k, o],
             device_id={"px": o},
             device_id_type=MESH,
         )
+
+    def hand_out(k):
+        def give(d, carry):
+            pick(split, slot_source, slot_weight, payload, ahead(d), ahead(d), 3 * k, 3 + k)
+            give_copy(ahead(d), k).start()
+            return carry
+
+        lax.fori_loop(0, n_px - 1, give, 0)
 
     loads[0].wait()
     south, north = columns([p[j] for j in range(levels)])
@@ -294,7 +304,7 @@
     st_rims[1] = south * A
     st_rims[2] = st[:, last, :] * A
     st_rims[3] = north * A
-    slot_count = payload.shape[2]
+    slot_count = payload.shape[3]
     find_slots(n_px, slot_count, owner, source, weight, slot_source, slot_weight)
 
     def ahead(d):
@@ -375,9 +385,9 @@
 
         @pl.when(t == SUBSTEPS - 1)
         def _():
-            for q, field in ((1, we), (2, wn), (3, wu)):
+            for q, field in enumerate((we, wn, wu)):
                 split_field(split, field, q)
-            pick(split, slot_source, slot_weight, payload, ahead(0), ahead(0), 1, 4)
+            hand_out(0)
 
         gw, gs, ge, gn = wind_ghosts(t)
 
@@ -399,23 +409,16 @@
 
     lax.fori_loop(0, SUBSTEPS, substep, 0)
 
-    split_field(split, p, 0)
-    pick(split, slot_source, slot_weight, payload, ahead(0), ahead(0), 0, 1)
-    give_copy(ahead(0)).start()
-
-    def hand_out(d, carry):
-        pick(split, slot_source, slot_weight, payload, ahead(d), ahead(d), 0, 4)
-        give_copy(ahead(d)).start()
-        return carry
-
-    lax.fori_loop(1, n_px - 1, hand_out, 0)
+    split_field(split, p, 3)
+    hand_out(1)
     pick(split, slot_source, slot_weight, arrived, ix, ix, 0, 4)
     total[...] = jnp.zeros(total.shape, jnp.float32)
     land(arrived, cell, ix, total)
 
     def bring_in(d, carry):
         o = lax.rem(ix + n_px - d - 1, n_px)
-        got(o).wait_recv()
+        got(o, 0).wait_recv()
+        got(o, 1).wait_recv()
         land(arrived, cell, o, total)
         return carry
 
@@ -424,7 +427,7 @@
     for g in range(groups):
         both = total[g * count : (g + 1) * count] + total[(groups + g) * count : (groups + g + 1) * count]
         for q in range(4):
-            latlon[q, :, g * BLOCK : (g + 1) * BLOCK] = both[q * levels : (q + 1) * levels]
+            latlon[(q + 1) % 4, :, g * BLOCK : (g + 1) * BLOCK] = both[q * levels : (q + 1) * levels]
 
     def drain(t, carry):
         for s in range(4):
@@ -435,7 +438,8 @@
     lax.fori_loop(0, SUBSTEPS, drain, 0)
 
     def sent(d, carry):
-        give_copy(ahead(d)).wait_send()
+        give_copy(ahead(d), 0).wait_send()
+        give_copy(ahead(d), 1).wait_send()
         return carry
 
     lax.fori_loop(0, n_px - 1, sent, 0)
@@ -489,12 +493,11 @@
 
 
 def pick(split, slot_source, slot_weight, dst, place, o, first, end):
-    rows, slot_count = dst.shape[1:]
+    _, _, quarter, slot_count = dst.shape
     tile = split.shape[1] // 4
     half = tile // 2
     width = min(BLOCK, slot_count)
     pieces = width // LANES
-    quarter = rows // 4
     at = slice(first * quarter * half, end * quarter * half)
 
     def joined(ref, b):
@@ -510,23 +513,27 @@
             split[at, :], jnp.concatenate([hot, hot], axis=0), preferred_element_type=jnp.float32
         )
         mask = jnp.where(iota((half, width), 0) == (y & (half - 1)), w, 0.0)
-        dst[place, first * quarter : end * quarter, pl.ds(pl.multiple_of(b * width, width), width)] = jnp.sum(
-            picked.reshape((end - first) * quarter, half, width) * mask[None], axis=1
-        )
+        taken = jnp.sum(picked.reshape((end - first) * quarter, half, width) * mask[None], axis=1)
+        for q in range(first, end):
+            dst[place, q, :, pl.ds(pl.multiple_of(b * width, width), width)] = taken[
+                (q - first) * quarter : (q - first + 1) * quarter
+            ]
         return carry
 
     lax.fori_loop(0, slot_count // width, step, 0)
 
 
 def land(arrived, cell, o, total):
-    count, slot_count = arrived.shape[1:]
+    _, parts, levels, slot_count = arrived.shape
+    count = parts * levels
     groups = total.shape[0] // (2 * count)
     width = min(4 * BLOCK, slot_count)
 
     def step(b, carry):
         at = pl.ds(pl.multiple_of(b * width, width), width)
-        c = cell[pl.ds(o, 1), at]
-        values = arrived[o, :, at]
+        row = o * (slot_count // LANES) + b * (width // LANES)
+        c = jnp.concatenate([cell[pl.ds(row + k, 1), :] for k in range(width // LANES)], axis=1)
+        values = jnp.concatenate([arrived[o, q, :, at] for q in range(parts)], axis=0)
         h = values.astype(jnp.bfloat16).astype(jnp.float32)
         group = c >> 8
         spread = [jnp.where(group == g, h, 0.0) for g in range(groups)]
@@ -580,7 +587,7 @@
             pltpu.VMEM((rows, LANES), i32),
             pltpu.VMEM((rows, LANES), i32),
             pltpu.VMEM((rows, LANES), f32),
-            pltpu.VMEM((owner_count, slot_count), i32),
+            pltpu.VMEM((slots // LANES, LANES), i32),
             pltpu.VMEM((n, 4, levels, tile), f32),
             pltpu.VMEM((n, 4, 4, levels, tile), f32),
             pltpu.VMEM((n, 4, 2 * levels, tile), f32),
@@ -595,8 +602,8 @@
             pltpu.VMEM((slots // LANES, LANES), i32),
             pltpu.VMEM((slots // LANES, LANES), f32),
             pltpu.VMEM((count * tile // 2, 4 * tile), jnp.bfloat16),
-            pltpu.VMEM((owner_count, count, slot_count), f32),
-            pltpu.VMEM((owner_count, count, slot_count), f32),
+            pltpu.VMEM((owner_count, 4, levels, slot_count), f32),
+            pltpu.VMEM((owner_count, 4, levels, slot_count), f32),
             pltpu.VMEM((2 * count * (cell_count // BLOCK), BLOCK), f32),
             dma((9,)),
             dma((n, 4)),
@@ -606,8 +613,8 @@
             dma((2, n)),
             dma((2, n)),
             dma((2,)),
-            dma((owner_count,)),
-            dma((owner_count,)),
+            dma((2, owner_count)),
+            dma((2, owner_count)),
         ],
         compiler_params=pltpu.CompilerParams(
             collective_id=0, has_side_effects=True, vmem_limit_bytes=60 * 2**20
@@ -622,7 +629,7 @@
         remap_owner.reshape(rows, LANES),
         remap_source.reshape(rows, LANES),
         remap_weight.reshape(rows, LANES),
-        latlon_cell.reshape(owner_count, slot_count),
+        latlon_cell.reshape(slots // LANES, LANES),
     )
 
 

time: 59.8 us -> 61.3 us (1.025)
  Pallas kernels: 55.1 us -> 58 us
  local copies, waits for them, and re-layouts: 3.75 us -> 2.36 us
    pallas_call x1, Pallas kernels: 55.1 us -> 58 us  [per_device(): pl.pallas_call(functools.partial(whole_kernel, sizes), out_shape=[jax.Sha...]
    reshape x1 -> x0, local copies, waits for them, and re-layouts: 1.39 us -> none  [per_device(): latlon_cell.reshape(owner_count, slot_count)]
where the time goes in v3:
time: 61.3 us; the launch traced here: 61 us
  Pallas kernels  58 us (95%)
  local copies, waits for them, and re-layouts  2.36 us (4%)
  between operations  0.65 us (1%)
    pallas_call x1, Pallas kernels, per_device(): pl.pallas_call(functools.partial(whole_kernel, sizes), out_shape=[jax.Sha...  58 us
    unnamed x4, local copies, waits for them, and re-layouts  2.36 us

profile of v3, /device:TPU:0, one launch (start us, length us, event | category | flops | bytes accessed | tf_op | source)
XLA Modules:
  0.0 61.0 jit_solution(6569259246621310816)
XLA Ops:
  0.6 58.0 %shard_map.113 = (f32[4,128,128]{2,1,0:T(8,128)}, f32[4,4,2048]{2,1,0:T(4,128)}) custom-call(s32[4,4,4]{2,1,0:T(4,128)} %edges.1, f32[4,128,128]{2,1,0:T(8,128)} %p_in.1, f32[4,128,128]{2,1,0:T(8,128)} %we_in.1, f32[4,128,128]{2,1,0:T(8,128)} %wn_in.1, f32[4,128,128]{2,1,0:T(8,128)} %wu_in.1, f32[4,128,128]{2,1,0:T(8,128)} %st_in.1, s32[32,128]{1,0:T(8,128)} %bitcast.5, ...), custom_call_target="tpu_custom_call" | custom-call | tf_op jit(solution)/shard_map/pallas_call | solution.py:574
  58.7 0.0 copy-start
  58.7 1.7 %copy.14 = f32[4,128,128]{2,1,0:T(8,128)} copy(f32[4,128,128]{2,1,0:T(8,128)} %get-tuple-element.4) | data formatting | bytes 524288
  60.4 0.0 copy-done
  60.4 0.7 %copy.15 = f32[4,4,2048]{2,1,0:T(4,128)} copy(f32[4,4,2048]{2,1,0:T(4,128)S(1)} %copy-done) | data formatting | bytes 262144
Async XLA Ops:
  58.7 1.7 %copy-start = (f32[4,4,2048]{2,1,0:T(4,128)S(1)}, f32[4,4,2048]{2,1,0:T(4,128)}, u32[]{:S(2)}) copy-start(f32[4,4,2048]{2,1,0:T(4,128)} %get-tuple-element.5) | copy-start | bytes 393220

commit v4 on v2

--- a/solution.py
+++ b/solution.py
@@ -525,7 +525,8 @@
 
     def step(b, carry):
         at = pl.ds(pl.multiple_of(b * width, width), width)
-        c = cell[pl.ds(o, 1), at]
+        row = o * (slot_count // LANES) + b * (width // LANES)
+        c = jnp.concatenate([cell[pl.ds(row + k, 1), :] for k in range(width // LANES)], axis=1)
         values = arrived[o, :, at]
         h = values.astype(jnp.bfloat16).astype(jnp.float32)
         group = c >> 8
@@ -580,7 +581,7 @@
             pltpu.VMEM((rows, LANES), i32),
             pltpu.VMEM((rows, LANES), i32),
             pltpu.VMEM((rows, LANES), f32),
-            pltpu.VMEM((owner_count, slot_count), i32),
+            pltpu.VMEM((slots // LANES, LANES), i32),
             pltpu.VMEM((n, 4, levels, tile), f32),
             pltpu.VMEM((n, 4, 4, levels, tile), f32),
             pltpu.VMEM((n, 4, 2 * levels, tile), f32),
@@ -622,7 +623,7 @@
         remap_owner.reshape(rows, LANES),
         remap_source.reshape(rows, LANES),
         remap_weight.reshape(rows, LANES),
-        latlon_cell.reshape(owner_count, slot_count),
+        latlon_cell.reshape(slots // LANES, LANES),
     )
 
 

time: 59.8 us -> 58.4 us (0.977)
  local copies, waits for them, and re-layouts: 3.75 us -> 2.36 us
    reshape x1 -> x0, local copies, waits for them, and re-layouts: 1.39 us -> none  [per_device(): latlon_cell.reshape(owner_count, slot_count)]
where the time goes in v4:
time: 58.4 us; the launch traced here: 58.2 us
  Pallas kernels  55.2 us (95%)
  local copies, waits for them, and re-layouts  2.36 us (4%)
  between operations  0.65 us (1%)
    pallas_call x1, Pallas kernels, per_device(): pl.pallas_call(functools.partial(whole_kernel, sizes), out_shape=[jax.Sha...  55.2 us
    unnamed x4, local copies, waits for them, and re-layouts  2.36 us

profile of v4, /device:TPU:0, one launch (start us, length us, event | category | flops | bytes accessed | tf_op | source)
XLA Modules:
  0.0 58.2 jit_solution(14771442220972615015)
XLA Ops:
  0.6 55.2 %shard_map.113 = (f32[4,128,128]{2,1,0:T(8,128)}, f32[4,4,2048]{2,1,0:T(4,128)}) custom-call(s32[4,4,4]{2,1,0:T(4,128)} %edges.1, f32[4,128,128]{2,1,0:T(8,128)} %p_in.1, f32[4,128,128]{2,1,0:T(8,128)} %we_in.1, f32[4,128,128]{2,1,0:T(8,128)} %wn_in.1, f32[4,128,128]{2,1,0:T(8,128)} %wu_in.1, f32[4,128,128]{2,1,0:T(8,128)} %st_in.1, s32[32,128]{1,0:T(8,128)} %bitcast.5, ...), custom_call_target="tpu_custom_call" | custom-call | tf_op jit(solution)/shard_map/pallas_call | solution.py:568
  55.8 0.0 copy-start
  55.8 1.7 %copy.14 = f32[4,128,128]{2,1,0:T(8,128)} copy(f32[4,128,128]{2,1,0:T(8,128)} %get-tuple-element.4) | data formatting | bytes 524288
  57.5 0.0 copy-done
  57.5 0.7 %copy.15 = f32[4,4,2048]{2,1,0:T(4,128)} copy(f32[4,4,2048]{2,1,0:T(4,128)S(1)} %copy-done) | data formatting | bytes 262144
Async XLA Ops:
  55.8 1.7 %copy-start = (f32[4,4,2048]{2,1,0:T(4,128)S(1)}, f32[4,4,2048]{2,1,0:T(4,128)}, u32[]{:S(2)}) copy-start(f32[4,4,2048]{2,1,0:T(4,128)} %get-tuple-element.5) | copy-start | bytes 393220
